TPU v7x, 32 devices: a whole 2x2x4 slice. The times are simulated.
32 devices in a mesh: dp: 8 (over y, x, core), ctx: 4 (over z).
Axes of the slice: x: 2, y: 2, z: 4, core: 2. Of those that a mesh axis runs over, the one named last changes fastest.
Arguments:
- hidden_in: bfloat16 [2, 8, 1024, 1024], P(None, 'dp', 'ctx'), may hold values from -6 to 6
- out_grad: bfloat16 [2, 8, 1024, 1024], P(None, 'dp', 'ctx'), may hold values from -6 to 6
- segment_ids: int32 [2, 8, 1024], P(None, 'dp', 'ctx'), may hold values from 0 to 5, as said below
- doc_positions: int32 [2, 8, 1024], P(None, 'dp', 'ctx'), may hold values from 0 to 1021, as said below
- attn_gain: bfloat16 [1024], P(('dp', 'ctx')), may hold values from 0.5 to 1.5
- head_gains: bfloat16 [128], P(('dp', 'ctx')), may hold values from 0.5 to 1.5
- w_query: bfloat16 [1024, 1024], P(('dp', 'ctx')), may hold values from -0.1875 to 0.1875
- w_key: bfloat16 [1024, 512], P(('dp', 'ctx')), may hold values from -0.1875 to 0.1875
- w_value: bfloat16 [1024, 512], P(('dp', 'ctx')), may hold values from -0.1875 to 0.1875
- w_out: bfloat16 [1024, 1024], P(('dp', 'ctx')), may hold values from -1.5 to 1.5
- ffn_gain: bfloat16 [1024], P(('dp', 'ctx')), may hold values from 0.5 to 1.5
- w_gate: bfloat16 [1024, 4608], P(('dp', 'ctx')), may hold values from -0.1875 to 0.1875
- w_up: bfloat16 [1024, 4608], P(('dp', 'ctx')), may hold values from -0.1875 to 0.1875
- w_down: bfloat16 [4608, 1024], P(('dp', 'ctx')), may hold values from -0.09375 to 0.09375
Outputs:
- block_out: bfloat16 [2, 8, 1024, 1024], P(None, 'dp', 'ctx')
- in_grad: bfloat16 [2, 8, 1024, 1024], P(None, 'dp', 'ctx')
- attn_gain_grad: float32 [1024], P(('dp', 'ctx'))
- head_gains_grad: float32 [128], P(('dp', 'ctx'))
- w_query_grad: float32 [1024, 1024], P(('dp', 'ctx'))
- w_key_grad: float32 [1024, 512], P(('dp', 'ctx'))
- w_value_grad: float32 [1024, 512], P(('dp', 'ctx'))
- w_out_grad: float32 [1024, 1024], P(('dp', 'ctx'))
- ffn_gain_grad: float32 [1024], P(('dp', 'ctx'))
- w_gate_grad: float32 [1024, 4608], P(('dp', 'ctx'))
- w_up_grad: float32 [1024, 4608], P(('dp', 'ctx'))
- w_down_grad: float32 [4608, 1024], P(('dp', 'ctx'))
Inputs may be any that keep to these rules, and one draw needn't show every extreme that they name: `segment_ids`: in each sequence the ids start at 0, rise by one at each new document and never fall. In one sequence of each index of the second dimension a single document starts within the first 256 tokens and ends within the last 256, the tokens before and after it forming one document each; in the sequence at index 0 of the second dimension that document runs from token 1 to token 1022, and the other sequence there packs documents of 200 tokens. The other sequences pack documents of 200 to 2000 tokens and at most 1022, the last one cut at the sequence's end. `doc_positions`: each token's place within its document, counting from 0 at the document's first token.
All inputs are finite; a program needn't handle non-finite values.
Results may differ from a plain program's by a relative error of at most 0.022.
Values may be sent and summed in bfloat16 or wider, within the bound.
No kernel may reach another device: no remote copies, remote signals or barrier semaphores. Data moves between devices by JAX's collectives and lax.ppermute only.
A program may use at most 320 MiB of HBM per device.

v0:
```python
import functools

import jax
import jax.numpy as jnp
from jax import lax
from jax.experimental import pallas as pl
from jax.experimental.pallas import tpu as pltpu
from jax.sharding import PartitionSpec as P

EPS = 1e-05
THETA = 1000000.0


def matmul(left, right):
    return jnp.dot(left, right, preferred_element_type=jnp.float32)


def left_trans(left, right):
    return lax.dot_general(
        left, right, (((0,), (0,)), ((), ())), preferred_element_type=jnp.float32
    )


def right_trans(left, right):
    return lax.dot_general(
        left, right, (((1,), (1,)), ((), ())), preferred_element_type=jnp.float32
    )


def norm_forward(values, gain):
    factor = lax.rsqrt(jnp.mean(values * values, -1, keepdims=True) + EPS)
    unit = values * factor
    return (unit * gain, unit, factor)


def norm_backward(incoming, unit, factor, gain):
    scaled = incoming * gain
    result = factor * (scaled - unit * jnp.mean(scaled * unit, -1, keepdims=True))
    return (result, incoming * unit)


def angles(places, half):
    freq = THETA ** (-(jnp.arange(half, dtype=jnp.float32) * 2.0 / (2 * half)))
    turn = places.astype(jnp.float32)[:, None] * freq[None, :]
    return (jnp.cos(turn)[:, None, :], jnp.sin(turn)[:, None, :])


def rotate(values, cosine, sine, sign):
    half = values.shape[-1] // 2
    first = values[..., :half]
    second = values[..., half:]
    return jnp.concatenate(
        [first * cosine - sign * second * sine, second * cosine + sign * first * sine], -1
    )


def fetch_weights(shards):
    return (
        lax.all_gather(shards[0], ("dp", "ctx"), axis=0, tiled=True),
        lax.all_gather(shards[1], ("dp", "ctx"), axis=0, tiled=True),
        lax.all_gather(shards[2], ("dp", "ctx"), axis=0, tiled=True),
        lax.all_gather(shards[3], ("dp", "ctx"), axis=0, tiled=True),
        lax.all_gather(shards[4], ("dp", "ctx"), axis=0, tiled=True),
        lax.all_gather(shards[5], ("dp", "ctx"), axis=0, tiled=True),
        lax.all_gather(shards[6], ("dp", "ctx"), axis=0, tiled=True),
        lax.all_gather(shards[7], ("dp", "ctx"), axis=0, tiled=True),
        lax.all_gather(shards[8], ("dp", "ctx"), axis=0, tiled=True),
        lax.all_gather(shards[9], ("dp", "ctx"), axis=0, tiled=True),
    )


def fetch_again(shards):
    return (
        lax.all_gather(shards[0], ("dp", "ctx"), axis=0, tiled=True),
        lax.all_gather(shards[1], ("dp", "ctx"), axis=0, tiled=True),
        lax.all_gather(shards[2], ("dp", "ctx"), axis=0, tiled=True),
        lax.all_gather(shards[3], ("dp", "ctx"), axis=0, tiled=True),
        lax.all_gather(shards[4], ("dp", "ctx"), axis=0, tiled=True),
        lax.all_gather(shards[5], ("dp", "ctx"), axis=0, tiled=True),
        lax.all_gather(shards[6], ("dp", "ctx"), axis=0, tiled=True),
        lax.all_gather(shards[7], ("dp", "ctx"), axis=0, tiled=True),
        lax.all_gather(shards[8], ("dp", "ctx"), axis=0, tiled=True),
        lax.all_gather(shards[9], ("dp", "ctx"), axis=0, tiled=True),
    )


def attention_forward(query_low, key_low, value_low, segments, again):
    rows, heads, head = query_low.shape
    kv_heads = key_low.shape[1] // head
    group = heads // kv_heads
    scale = head ** (-0.5)
    grouped = query_low.reshape(rows, kv_heads, group, head)
    query_index = lax.axis_index("ctx") * rows + jnp.arange(rows, dtype=jnp.int32)

    def visit(carry, piece):
        highest, total, summed = carry
        key_piece, value_piece, segment_piece = piece
        width = key_piece.shape[0]
        key_heads = key_piece.reshape(width, kv_heads, head)
        value_heads = value_piece.reshape(width, kv_heads, head)
        scores = (
            jnp.einsum("qkgd,skd->kgqs", grouped, key_heads, preferred_element_type=jnp.float32)
            * scale
        )
        key_index = jnp.arange(width, dtype=jnp.int32)
        allowed = (segments[:, None] == segment_piece[None, :]) & (
            query_index[:, None] >= key_index[None, :]
        )
        scores = jnp.where(allowed, scores, -1e30)
        peak = jnp.maximum(highest, jnp.max(scores, -1))
        weight = jnp.where(allowed, jnp.exp(scores - peak[..., None]), 0.0)
        total = jnp.sum(weight, -1)
        summed = jnp.einsum(
            "kgqs,skd->qkgd",
            weight.astype(jnp.bfloat16),
            value_heads,
            preferred_element_type=jnp.float32,
        )
        return (peak, total, summed)

    initial = (
        jnp.full((kv_heads, group, rows), -1e30, jnp.float32),
        jnp.zeros((kv_heads, group, rows), jnp.float32),
        jnp.zeros((rows, kv_heads, group, head), jnp.float32),
    )
    if again:
        highest, total, summed = visit(
            initial,
            (
                lax.all_gather(key_low, "ctx", axis=0, tiled=True),
                lax.all_gather(value_low, "ctx", axis=0, tiled=True),
                lax.all_gather(segments, "ctx", axis=0, tiled=True),
            ),
        )
    else:
        highest, total, summed = visit(
            initial,
            (
                lax.all_gather(key_low, "ctx", axis=0, tiled=True),
                lax.all_gather(value_low, "ctx", axis=0, tiled=True),
                lax.all_gather(segments, "ctx", axis=0, tiled=True),
            ),
        )
    attended = (summed / jnp.transpose(total, (2, 0, 1))[..., None]).reshape(rows, heads, head)
    return (attended, highest + jnp.log(total))


def forward(values_row, segments, places, weights, again):
    attn_gain, head_gains, w_query, w_key, w_value, w_out, ffn_gain, w_gate, w_up, w_down = weights
    rows = values_row.shape[0]
    head = head_gains.shape[0] // 2
    heads = w_query.shape[1] // head
    kv_heads = w_key.shape[1] // head
    gains = head_gains.astype(jnp.float32)
    state = {}
    state["values"] = values_row.astype(jnp.float32)
    normed, state["x_unit"], state["x_factor"] = norm_forward(
        state["values"], attn_gain.astype(jnp.float32)
    )
    state["a_low"] = normed.astype(jnp.bfloat16)
    query = matmul(state["a_low"], w_query).reshape(rows, heads, head)
    keys = matmul(state["a_low"], w_key).reshape(rows, kv_heads, head)
    state["value_low"] = matmul(state["a_low"], w_value).astype(jnp.bfloat16)
    state["cosine"], state["sine"] = angles(places, head // 2)
    query_normed, state["q_unit"], state["q_factor"] = norm_forward(query, gains[:head])
    key_normed, state["k_unit"], state["k_factor"] = norm_forward(keys, gains[head:])
    state["query_low"] = rotate(query_normed, state["cosine"], state["sine"], 1.0).astype(
        jnp.bfloat16
    )
    state["key_low"] = (
        rotate(key_normed, state["cosine"], state["sine"], 1.0)
        .astype(jnp.bfloat16)
        .reshape(rows, kv_heads * head)
    )
    state["attended"], state["log_total"] = attention_forward(
        state["query_low"], state["key_low"], state["value_low"], segments, again
    )
    state["attended_low"] = state["attended"].astype(jnp.bfloat16).reshape(rows, heads * head)
    hidden = state["values"] + matmul(state["attended_low"], w_out)
    normed_two, state["h_unit"], state["h_factor"] = norm_forward(
        hidden, ffn_gain.astype(jnp.float32)
    )
    state["b_low"] = normed_two.astype(jnp.bfloat16)
    state["gate"] = matmul(state["b_low"], w_gate)
    state["upper"] = matmul(state["b_low"], w_up)
    state["act_low"] = (jax.nn.silu(state["gate"]) * state["upper"]).astype(jnp.bfloat16)
    state["output"] = hidden + matmul(state["act_low"], w_down)
    return state


def backward(grad_row, segments, weights, state):
    attn_gain, head_gains, w_query, w_key, w_value, w_out, ffn_gain, w_gate, w_up, w_down = weights
    query_low = state["query_low"]
    rows, heads, head = query_low.shape
    kv_heads = state["key_low"].shape[1] // head
    group = heads // kv_heads
    scale = head ** (-0.5)
    gains = head_gains.astype(jnp.float32)
    incoming = grad_row.astype(jnp.float32)
    down_low = incoming.astype(jnp.bfloat16)
    g_down = left_trans(state["act_low"], down_low)
    d_act = right_trans(down_low, w_down)
    sigma = jax.nn.sigmoid(state["gate"])
    d_upper = (d_act * state["gate"] * sigma).astype(jnp.bfloat16)
    d_gate = (d_act * state["upper"] * sigma * (1.0 + state["gate"] * (1.0 - sigma))).astype(
        jnp.bfloat16
    )
    g_gate = left_trans(state["b_low"], d_gate)
    g_up = left_trans(state["b_low"], d_upper)
    d_normed = right_trans(d_gate, w_gate) + right_trans(d_upper, w_up)
    d_hidden, terms = norm_backward(
        d_normed, state["h_unit"], state["h_factor"], ffn_gain.astype(jnp.float32)
    )
    g_ffn = jnp.sum(terms, 0)
    d_hidden = incoming + d_hidden
    branch_low = d_hidden.astype(jnp.bfloat16)
    g_out = left_trans(state["attended_low"], branch_low)
    d_attended = (
        right_trans(branch_low, w_out).astype(jnp.bfloat16).reshape(rows, kv_heads, group, head)
    )
    delta = jnp.sum(
        d_attended.astype(jnp.float32) * state["attended"].reshape(rows, kv_heads, group, head), -1
    )
    delta = jnp.transpose(delta, (1, 2, 0))
    log_total = state["log_total"]
    grouped = query_low.reshape(rows, kv_heads, group, head)
    query_index = lax.axis_index("ctx") * rows + jnp.arange(rows, dtype=jnp.int32)
    key_piece = lax.all_gather(state["key_low"], "ctx", axis=0, tiled=True)
    value_piece = lax.all_gather(state["value_low"], "ctx", axis=0, tiled=True)
    segment_piece = lax.all_gather(segments, "ctx", axis=0, tiled=True)
    width = key_piece.shape[0]
    key_heads = key_piece.reshape(width, kv_heads, head)
    value_heads = value_piece.reshape(width, kv_heads, head)
    scores = (
        jnp.einsum("qkgd,skd->kgqs", grouped, key_heads, preferred_element_type=jnp.float32) * scale
    )
    key_index = jnp.arange(width, dtype=jnp.int32)
    allowed = (segments[:, None] == segment_piece[None, :]) & (
        query_index[:, None] >= key_index[None, :]
    )
    probs = jnp.where(allowed, jnp.exp(scores - log_total[..., None]), 0.0)
    d_probs = jnp.einsum(
        "qkgd,skd->kgqs", d_attended, value_heads, preferred_element_type=jnp.float32
    )
    d_scores = (probs * (d_probs - delta[..., None])).astype(jnp.bfloat16)
    d_query = (
        jnp.einsum("kgqs,skd->qkgd", d_scores, key_heads, preferred_element_type=jnp.float32)
        * scale
    )
    key_part = (
        jnp.einsum("kgqs,qkgd->skd", d_scores, grouped, preferred_element_type=jnp.float32) * scale
    )
    value_part = jnp.einsum(
        "kgqs,qkgd->skd", probs.astype(jnp.bfloat16), d_attended, preferred_element_type=jnp.float32
    )
    d_keys = key_part.reshape(width, kv_heads * head)
    d_values = value_part.reshape(width, kv_heads * head)
    d_query, d_keys_all, d_values_all = (d_query, d_keys, d_values)
    d_keys, d_values = (
        lax.psum_scatter(
            d_keys_all.astype(jnp.bfloat16), "ctx", scatter_dimension=0, tiled=True
        ).astype(jnp.float32),
        lax.psum_scatter(
            d_values_all.astype(jnp.bfloat16), "ctx", scatter_dimension=0, tiled=True
        ).astype(jnp.float32),
    )
    d_query = rotate(d_query.reshape(rows, heads, head), state["cosine"], state["sine"], -1.0)
    d_query, query_terms = norm_backward(d_query, state["q_unit"], state["q_factor"], gains[:head])
    d_keys = rotate(d_keys.reshape(rows, kv_heads, head), state["cosine"], state["sine"], -1.0)
    d_keys, key_terms = norm_backward(d_keys, state["k_unit"], state["k_factor"], gains[head:])
    g_heads = jnp.concatenate([jnp.sum(query_terms, (0, 1)), jnp.sum(key_terms, (0, 1))])
    query_grad_low = d_query.astype(jnp.bfloat16).reshape(rows, heads * head)
    key_grad_low = d_keys.astype(jnp.bfloat16).reshape(rows, kv_heads * head)
    value_grad_low = d_values.astype(jnp.bfloat16)
    g_query = left_trans(state["a_low"], query_grad_low)
    g_key = left_trans(state["a_low"], key_grad_low)
    g_value = left_trans(state["a_low"], value_grad_low)
    d_inner = (
        right_trans(query_grad_low, w_query)
        + right_trans(key_grad_low, w_key)
        + right_trans(value_grad_low, w_value)
    )
    d_input, terms = norm_backward(
        d_inner, state["x_unit"], state["x_factor"], attn_gain.astype(jnp.float32)
    )
    g_attn = jnp.sum(terms, 0)
    in_grad = (d_hidden + d_input).astype(jnp.bfloat16)
    return (in_grad, (g_attn, g_heads, g_query, g_key, g_value, g_out, g_ffn, g_gate, g_up, g_down))


def on_device(
    hidden_in,
    out_grad,
    segment_ids,
    doc_positions,
    attn_gain,
    head_gains,
    w_query,
    w_key,
    w_value,
    w_out,
    ffn_gain,
    w_gate,
    w_up,
    w_down,
):
    shards = (attn_gain, head_gains, w_query, w_key, w_value, w_out, ffn_gain, w_gate, w_up, w_down)
    micro = hidden_in.shape[0]
    outputs = []
    for micro_index in range(micro):
        weights = fetch_weights(shards)
        state = forward(
            hidden_in[micro_index, 0],
            segment_ids[micro_index, 0],
            doc_positions[micro_index, 0],
            weights,
            False,
        )
        outputs.append(state["output"].astype(jnp.bfloat16))
    in_grads = []
    totals = None
    for micro_index in range(micro):
        weights = fetch_again(shards)
        state = forward(
            hidden_in[micro_index, 0],
            segment_ids[micro_index, 0],
            doc_positions[micro_index, 0],
            weights,
            True,
        )
        in_grad, grads = backward(
            out_grad[micro_index, 0], segment_ids[micro_index, 0], weights, state
        )
        in_grads.append(in_grad)
        if totals is None:
            totals = grads
        else:
            totals = tuple((left + right for left, right in zip(totals, grads)))
    totals = lax.psum_scatter(totals, ("dp", "ctx"), scatter_dimension=0, tiled=True)
    block_out = jnp.stack(outputs)[:, None]
    input_grads = jnp.stack(in_grads)[:, None]
    return (
        block_out,
        input_grads,
        totals[0],
        totals[1],
        totals[2],
        totals[3],
        totals[4],
        totals[5],
        totals[6],
        totals[7],
        totals[8],
        totals[9],
    )


CORE, SIDE, HIGH = 1, 2, 4


def flip(array, bits):
    count = lax.axis_size("dp")
    return lax.ppermute(array, "dp", [(i, i ^ bits) for i in range(count)])


def spin(array):
    count = lax.axis_size("ctx")
    return lax.ppermute(array, "ctx", [(i, (i + 1) % count) for i in range(count)])


def hold(*arrays):
    return lax.optimization_barrier(arrays)


def choose(bit, zero, one):
    return jnp.where(bit == 0, zero, one)


def pick(array, index, axis=0):
    return lax.dynamic_index_in_dim(array, index, axis, keepdims=False)


def put(buffer, array, *place):
    index = place + (0,) * (buffer.ndim - len(place))
    shape = (1,) * (buffer.ndim - array.ndim) + array.shape
    return lax.dynamic_update_slice(buffer, array.reshape(shape), index)


def place_kernel(splits, count, slots_ref, *refs):
    pieces, outs = refs[:count], refs[count:]
    at = 0
    for piece in pieces:
        for part in range(len(splits)):
            outs[splits[part]][slots_ref[at]] = piece[part]
            at += 1


def placed(pieces, splits, slots, counts):
    shape = pieces[0].shape
    return pl.pallas_call(
        functools.partial(place_kernel, splits, len(pieces)),
        in_specs=[pl.BlockSpec(memory_space=pltpu.SMEM)]
        + [pl.BlockSpec(memory_space=pltpu.VMEM)] * len(pieces),
        out_specs=[pl.BlockSpec(memory_space=pltpu.VMEM)] * len(counts),
        out_shape=[
            jax.ShapeDtypeStruct((count,) + shape[1:], pieces[0].dtype) for count in counts
        ],
        compiler_params=pltpu.CompilerParams(vmem_limit_bytes=40 * 2**20),
    )(jnp.stack(slots).astype(jnp.int32), *pieces)


def block_kernel(slots_ref, own_ref, core_ref, side_ref, down_ref, out_ref):
    rows = own_ref.shape[1]
    for member, ref, first in ((0, own_ref, 0), (1, core_ref, 1), (2, side_ref, 0), (3, side_ref, 2)):
        for part in range(2):
            start = pl.multiple_of((part * 4 + slots_ref[member]) * rows, rows)
            out_ref[pl.ds(start, rows), :] = ref[first + part]
    out_ref[8 * rows :, : down_ref.shape[1]] = down_ref[...]
    out_ref[8 * rows :, down_ref.shape[1] :] = jnp.zeros_like(
        out_ref[8 * rows :, down_ref.shape[1] :]
    )


def unit_block(slots, own, from_core, from_side, down):
    rows, columns = own.shape[1:]
    shape = (8 * rows + down.shape[0], columns)
    return pl.pallas_call(
        block_kernel,
        in_specs=[pl.BlockSpec(memory_space=pltpu.SMEM)]
        + [pl.BlockSpec(memory_space=pltpu.VMEM)] * 4,
        out_specs=pl.BlockSpec(memory_space=pltpu.VMEM),
        out_shape=jax.ShapeDtypeStruct(shape, own.dtype),
    )(jnp.stack(slots).astype(jnp.int32), own, from_core, from_side, down)


def unit_kernel(chunk, ctx_count, tiles, rows, slots_ref, *refs):
    pieces, refs = refs[: 2 * ctx_count], refs[2 * ctx_count :]
    b_refs, df_refs = refs[:2], refs[2:4]
    act_ref, pre_ref, all_b_ref, all_df_ref = refs[-12:-8]
    db_refs, out_refs, (w_ref, down_ref, b_ref, df_ref) = refs[-8:-6], refs[-6:-4], refs[-4:]
    mid = pieces[0].shape[1]
    width = down_ref.shape[1]
    down_rows = pieces[0].shape[0] - 8 * rows
    tile = pl.program_id(0)

    @pl.when(tile == 0)
    def _():
        high = slots_ref[ctx_count]
        for step in range(ctx_count):
            place = slots_ref[step]
            for far in range(2):
                piece = pieces[2 * step + far]
                for member in range(4):
                    first = ((far * 4 + member) * ctx_count + place) * rows
                    to = pl.ds(pl.multiple_of(first, rows), rows)
                    w_ref[to, :mid] = piece[member * rows : (member + 1) * rows, :]
                    w_ref[to, mid:] = piece[(4 + member) * rows : (5 + member) * rows, :]
                half = high if far == 0 else 1 - high
                first = (half * ctx_count + place) * down_rows
                to = pl.ds(pl.multiple_of(first, 16), down_rows)
                down_ref[to, :] = piece[8 * rows :, :width]

    for which in range(2):

        @pl.when(tile // tiles == which)
        def _(which=which):
            b_ref[...] = b_refs[which][...]
            df_ref[...] = df_refs[which][...]

    b, df = b_ref[...], df_ref[...]
    all_b_ref[...] = b
    all_df_ref[...] = df
    db, out = 0.0, 0.0
    for first, last in ((0, chunk), (chunk, mid)):
        here, there = slice(first, last), slice(mid + first, mid + last)
        gate = jnp.dot(b, w_ref[:, here], preferred_element_type=jnp.float32)
        upper = jnp.dot(b, w_ref[:, there], preferred_element_type=jnp.float32)
        d_act = nt(df, down_ref[here, :])
        sigma = 1.0 / (1.0 + jnp.exp(-gate))
        silu = gate * sigma
        act = (silu * upper).astype(jnp.bfloat16)
        d_upper = (d_act * silu).astype(jnp.bfloat16)
        d_gate = (d_act * upper * sigma * (1.0 + gate * (1.0 - sigma))).astype(jnp.bfloat16)
        act_ref[:, here] = act
        pre_ref[:, here] = d_gate
        pre_ref[:, there] = d_upper
        db += nt(d_gate, w_ref[:, here]) + nt(d_upper, w_ref[:, there])
        out += jnp.dot(act, down_ref[here, :], preferred_element_type=jnp.float32)
    for which in range(2):

        @pl.when(tile // tiles == which)
        def _(which=which):
            db_refs[which][...] = db.astype(jnp.bfloat16)
            out_refs[which][...] = out.astype(jnp.bfloat16)


def feed_forward(slots, pieces, rows, b_parts, df_parts, size, begin, left):
    tokens, width = b_parts[0].shape
    mid = pieces[0].shape[1]
    down_rows = pieces[0].shape[0] - 8 * rows
    tiles = tokens // size
    once = lambda array: pl.BlockSpec(
        array.shape, lambda t: (0,) * array.ndim, pipeline_mode=pl.Buffered(1)
    )

    def part(which):
        return pl.BlockSpec((size, width), lambda t: (jnp.clip(t - which * tiles, 0, tiles - 1), 0))

    def tiled(count, first):
        return pl.BlockSpec((size, count), lambda t: (first + t, 0))

    first = begin * tiles
    first_left = 1 + len(pieces) + 4
    full = lambda count: jax.ShapeDtypeStruct((4 * tokens, count), jnp.bfloat16)
    half = jax.ShapeDtypeStruct((tokens, width), jnp.bfloat16)
    return pl.pallas_call(
        functools.partial(unit_kernel, mid // 512 * 256, len(pieces) // 2, tiles, rows),
        grid=(2 * tiles,),
        in_specs=[pl.BlockSpec(memory_space=pltpu.SMEM)]
        + [once(array) for array in pieces]
        + [part(which) for which in range(2)] * 2
        + [pl.BlockSpec(memory_space=pl.ANY)] * len(left),
        out_specs=[tiled(mid, first), tiled(2 * mid, first), tiled(width, first), tiled(width, first)]
        + [part(which) for which in range(2)] * 2,
        out_shape=[full(mid), full(2 * mid), full(width), full(width)] + [half] * 4,
        input_output_aliases={first_left + at: at for at in range(len(left))},
        scratch_shapes=[
            pltpu.VMEM((width, 2 * mid), jnp.bfloat16),
            pltpu.VMEM((len(pieces) * down_rows, width), jnp.bfloat16),
            pltpu.VMEM((size, width), jnp.bfloat16),
            pltpu.VMEM((size, width), jnp.bfloat16),
        ],
        compiler_params=pltpu.CompilerParams(vmem_limit_bytes=58 * 2**20),
        cost_estimate=pl.CostEstimate(flops=10 * tokens * mid * width, bytes_accessed=0, transcendentals=0),
    )(jnp.stack(slots).astype(jnp.int32), *pieces, *b_parts, *df_parts, *left)


def spread_kernel(ctx_count, rows, slots_ref, ffn_ref, down_ref, *outs):
    mid = ffn_ref.shape[1] // 2
    width = down_ref.shape[1]
    down_rows = down_ref.shape[0] // (2 * ctx_count)
    high = slots_ref[ctx_count]
    for far in range(2):
        half = high if far == 0 else 1 - high
        for step in range(ctx_count):
            place = slots_ref[step]
            out = outs[far * ctx_count + step]
            for member in range(4):
                first = ((far * 4 + member) * ctx_count + place) * rows
                here = pl.ds(pl.multiple_of(first, rows), rows)
                out[member * rows : (member + 1) * rows, :] = ffn_ref[here, :mid]
                out[(4 + member) * rows : (5 + member) * rows, :] = ffn_ref[here, mid:]
            first = (half * ctx_count + place) * down_rows
            here = pl.ds(pl.multiple_of(first, 16), down_rows)
            out[8 * rows :, :width] = down_ref[here, :]
            out[8 * rows :, width:] = jnp.zeros_like(out[8 * rows :, width:])


def spread_units(slots, ffn, down, rows, ctx_count):
    shape = (8 * rows + down.shape[0] // (2 * ctx_count), ffn.shape[1] // 2)
    return pl.pallas_call(
        functools.partial(spread_kernel, ctx_count, rows),
        in_specs=[pl.BlockSpec(memory_space=pltpu.SMEM)]
        + [pl.BlockSpec(memory_space=pltpu.VMEM)] * 2,
        out_specs=[pl.BlockSpec(memory_space=pltpu.VMEM)] * (2 * ctx_count),
        out_shape=[jax.ShapeDtypeStruct(shape, ffn.dtype)] * (2 * ctx_count),
        compiler_params=pltpu.CompilerParams(vmem_limit_bytes=40 * 2**20),
        cost_estimate=pl.CostEstimate(flops=10**6, bytes_accessed=0, transcendentals=0),
    )(jnp.stack(slots).astype(jnp.int32), ffn, down)


def joined(*arrays):
    buffer = jnp.zeros((len(arrays),) + arrays[0].shape, arrays[0].dtype)
    for at, array in enumerate(arrays):
        buffer = put(buffer, array, at)
    return buffer


def order(bit, own, other):
    buffer = jnp.zeros((2,) + own.shape, own.dtype)
    return put(put(buffer, own, bit), other, 1 - bit)


def swap_halves(bit, array, axis):
    low, high = jnp.split(array, 2, axis)
    return choose(bit, array, jnp.concatenate([high, low], axis))


def half_of(bit, array, axis):
    low, high = jnp.split(array, 2, axis)
    return choose(bit, low, high)


def exchange(array, target, index_of):
    dp_count, ctx_count = lax.axis_size("dp"), lax.axis_size("ctx")
    me = lax.axis_index("dp") * ctx_count + lax.axis_index("ctx")
    came, kept = [], []
    for turn in range(2):
        pairs, stay = [], []
        for dp in range(dp_count):
            for z in range(ctx_count):
                to = target(dp, z, turn)
                if to == (dp, z):
                    stay.append(dp * ctx_count + z)
                else:
                    pairs.append((dp * ctx_count + z, to[0] * ctx_count + to[1]))
        piece = pick(array, index_of(turn))
        came.append(lax.ppermute(piece, ("dp", "ctx"), pairs))
        mine = functools.reduce(jnp.logical_or, [me == which for which in stay]) if stay else None
        kept.append((piece, mine))
    return came, kept


def settled(came, kept):
    return [
        got if mine is None else jnp.where(mine, piece, got)
        for got, (piece, mine) in zip(came, kept)
    ]


def spread(array):
    ctx = lax.axis_index("ctx")

    def target(dp, z, turn):
        return dp // 2 * 2 + z // 2, 2 * ((z + turn) % 2) + dp % 2

    return exchange(array, target, lambda turn: (ctx + turn) % 2)


def unspread(array):
    ctx = lax.axis_index("ctx")

    def target(dp, z, turn):
        return dp // 2 * 2 + z % 2, 2 * (dp % 2) + (z // 2 + turn) % 2

    return exchange(array, target, lambda turn: (ctx // 2 + turn) % 2)


def swap_gather(array, bit_value, bit):
    return order(bit_value, array, flip(array, bit))


def total_low(left, right):
    return (left.astype(jnp.float32) + right.astype(jnp.float32)).astype(jnp.bfloat16)


def nt(left, right):
    return lax.dot_general(
        left, right, (((1,), (1,)), ((), ())), preferred_element_type=jnp.float32
    )


def set_bias(bias_ref, seg_row_ref, seg_col_ref, block):
    size = bias_ref.shape[0]
    for first in range(0, size, block):
        for key in range(0, first + block, block):
            allowed = seg_col_ref[key : key + block, :] == seg_row_ref[:, first : first + block]
            if key == first:
                keys = lax.broadcasted_iota(jnp.int32, (block, block), 0)
                queries = lax.broadcasted_iota(jnp.int32, (block, block), 1)
                allowed = jnp.logical_and(allowed, keys <= queries)
            bias_ref[key : key + block, first : first + block] = jnp.where(allowed, 0.0, -1e30)


def turned(values, gain, cosine, sine):
    half = values.shape[0] // 2
    factor = lax.rsqrt(jnp.mean(values * values, 0, keepdims=True) + EPS)
    normed = values * factor * gain
    first, second = normed[:half], normed[half:]
    return jnp.concatenate([first * cosine - second * sine, second * cosine + first * sine], 0)


def turned_back(incoming, values, gain, cosine, sine):
    half = values.shape[0] // 2
    first, second = incoming[:half], incoming[half:]
    incoming = jnp.concatenate(
        [first * cosine + second * sine, second * cosine - first * sine], 0
    )
    factor = lax.rsqrt(jnp.mean(values * values, 0, keepdims=True) + EPS)
    unit = values * factor
    terms = jnp.sum(incoming * unit, 1, keepdims=True)
    scaled = incoming * gain
    return factor * (scaled - unit * jnp.mean(scaled * unit, 0, keepdims=True)), terms


def forward_kernel(
    block, q_ref, kv_ref, cos_ref, sin_ref, gain_ref, row_ref, col_ref,
    o_ref, log_ref, qr_ref, kvr_ref, bias_ref
):
    head = kv_ref.shape[0] // 2
    size = kv_ref.shape[1]
    scale = head ** (-0.5)

    @pl.when(pl.program_id(0) == 0)
    def _():
        set_bias(bias_ref, row_ref, col_ref, block)

    cosine, sine = cos_ref[...], sin_ref[...]
    keys = turned(kv_ref[:head, :], gain_ref[1], cosine, sine)
    kvr_ref[:head, :] = keys.astype(jnp.bfloat16)
    keys = keys.T.astype(jnp.bfloat16)
    values = kv_ref[head:, :].astype(jnp.bfloat16)
    kvr_ref[head:, :] = values
    for which in range(q_ref.shape[0] // head):
        rows = slice(which * head, (which + 1) * head)
        query = turned(q_ref[rows, :], gain_ref[0], cosine, sine).astype(jnp.bfloat16)
        qr_ref[rows, :] = query
        for first in range(0, size, block):
            here = slice(first, first + block)
            total = jnp.zeros((1, block), jnp.float32)
            summed = jnp.zeros((head, block), jnp.float32)
            for key in range(0, first + block, block):
                there = slice(key, key + block)
                scores = jnp.dot(keys[there], query[:, here], preferred_element_type=jnp.float32)
                weight = jnp.exp(scores * scale + bias_ref[there, here])
                total += jnp.sum(weight, 0, keepdims=True)
                summed += jnp.dot(
                    values[:, there],
                    weight.astype(jnp.bfloat16),
                    preferred_element_type=jnp.float32,
                )
            o_ref[rows, here] = summed / total
            log_ref[0, which : which + 1, here] = jnp.log(total)


def backward_kernel(
    block, q_ref, kv_ref, qr_ref, kvr_ref, do_ref, o_ref, log_ref, cos_ref, sin_ref,
    gain_ref, row_ref, col_ref, dq_ref, dkv_ref, gains_ref, bias_ref, dkey_ref, dvalue_ref
):
    head = kv_ref.shape[0] // 2
    size = kv_ref.shape[1]
    scale = head ** (-0.5)

    @pl.when(pl.program_id(0) == 0)
    def _():
        set_bias(bias_ref, row_ref, col_ref, block)
        gains_ref[...] = jnp.zeros_like(gains_ref)

    cosine, sine = cos_ref[...], sin_ref[...]
    keys_t = kvr_ref[:head, :]
    keys = keys_t.astype(jnp.float32).T.astype(jnp.bfloat16)
    values = kvr_ref[head:, :].astype(jnp.float32).T.astype(jnp.bfloat16)
    dkey_ref[...] = jnp.zeros_like(dkey_ref)
    dvalue_ref[...] = jnp.zeros_like(dvalue_ref)
    found = []
    for which in range(q_ref.shape[0] // head):
        rows = slice(which * head, (which + 1) * head)
        query = qr_ref[rows, :]
        grad = do_ref[rows, :]
        delta = jnp.sum(grad.astype(jnp.float32) * o_ref[rows, :], 0, keepdims=True)
        pieces = []
        for first in range(0, size, block):
            here = slice(first, first + block)
            dquery = jnp.zeros((head, block), jnp.float32)
            for key in range(0, first + block, block):
                there = slice(key, key + block)
                scores = jnp.dot(keys[there], query[:, here], preferred_element_type=jnp.float32)
                probs = jnp.exp(
                    scores * scale + (bias_ref[there, here] - log_ref[0, which : which + 1, here])
                )
                dprobs = jnp.dot(values[there], grad[:, here], preferred_element_type=jnp.float32)
                dscores = (probs * (dprobs - delta[:, here])).astype(jnp.bfloat16)
                dquery += jnp.dot(keys_t[:, there], dscores, preferred_element_type=jnp.float32)
                dkey_ref[:, there] += nt(query[:, here], dscores)
                dvalue_ref[:, there] += nt(grad[:, here], probs.astype(jnp.bfloat16))
            pieces.append(dquery * scale)
        dquery, terms = turned_back(
            jnp.concatenate(pieces, 1), q_ref[rows, :], gain_ref[0], cosine, sine
        )
        found.append(dquery)
        gains_ref[0] += terms
    dq_ref[...] = jnp.concatenate(found, 0).T.astype(jnp.bfloat16)
    dkey, terms = turned_back(dkey_ref[...] * scale, kv_ref[:head, :], gain_ref[1], cosine, sine)
    dkv_ref[...] = jnp.concatenate([dkey, dvalue_ref[...]], 0).T.astype(jnp.bfloat16)
    gains_ref[1] += terms


def whole_spec(*shape):
    return pl.BlockSpec(shape, lambda i: (0,) * len(shape))


def attend(raw, cosine, sine, gains, segments, kv_own, head, block):
    size = raw.shape[1]
    group = raw.shape[0] // head // kv_own - 2
    query = pl.BlockSpec((group * head, size), lambda i: (i, 0))
    kv_at = group * kv_own // 2
    return pl.pallas_call(
        functools.partial(forward_kernel, block),
        grid=(kv_own,),
        in_specs=[
            query,
            pl.BlockSpec((2 * head, size), lambda i: (kv_at + i, 0)),
            whole_spec(head // 2, size),
            whole_spec(head // 2, size),
            whole_spec(2, head, 1),
            whole_spec(1, size),
            whole_spec(size, 1),
        ],
        out_specs=[
            query,
            pl.BlockSpec((1, group, size), lambda i: (i, 0, 0)),
            query,
            pl.BlockSpec((2 * head, size), lambda i: (i, 0)),
        ],
        out_shape=[
            jax.ShapeDtypeStruct((kv_own * group * head, size), jnp.float32),
            jax.ShapeDtypeStruct((kv_own, group, size), jnp.float32),
            jax.ShapeDtypeStruct((kv_own * group * head, size), jnp.bfloat16),
            jax.ShapeDtypeStruct((kv_own * 2 * head, size), jnp.bfloat16),
        ],
        scratch_shapes=[pltpu.VMEM((size, size), jnp.float32)],
        compiler_params=pltpu.CompilerParams(vmem_limit_bytes=58 * 2**20),
        cost_estimate=pl.CostEstimate(flops=10**6, bytes_accessed=0, transcendentals=0),
    )(raw, raw, cosine, sine, gains, segments[None, :], segments[:, None])


def attend_back(
    raw, turned_q, turned_kv, grad, attended, logs, cosine, sine, gains, segments,
    kv_own, head, block, begin, count
):
    size = raw.shape[1]
    group = raw.shape[0] // head // kv_own - 2
    query = pl.BlockSpec((group * head, size), lambda i: (begin + i, 0))
    kv_at = group * kv_own // 2 + begin
    return pl.pallas_call(
        functools.partial(backward_kernel, block),
        grid=(count,),
        in_specs=[
            query,
            pl.BlockSpec((2 * head, size), lambda i: (kv_at + i, 0)),
            query,
            pl.BlockSpec((2 * head, size), lambda i: (begin + i, 0)),
            query,
            query,
            pl.BlockSpec((1, group, size), lambda i: (begin + i, 0, 0)),
            whole_spec(head // 2, size),
            whole_spec(head // 2, size),
            whole_spec(2, head, 1),
            whole_spec(1, size),
            whole_spec(size, 1),
        ],
        out_specs=[
            pl.BlockSpec((size, group * head), lambda i: (0, i)),
            pl.BlockSpec((size, 2 * head), lambda i: (0, i)),
            whole_spec(2, head, 1),
        ],
        out_shape=[
            jax.ShapeDtypeStruct((size, count * group * head), jnp.bfloat16),
            jax.ShapeDtypeStruct((size, count * 2 * head), jnp.bfloat16),
            jax.ShapeDtypeStruct((2, head, 1), jnp.float32),
        ],
        scratch_shapes=[
            pltpu.VMEM((size, size), jnp.float32),
            pltpu.VMEM((head, size), jnp.float32),
            pltpu.VMEM((head, size), jnp.float32),
        ],
        compiler_params=pltpu.CompilerParams(vmem_limit_bytes=58 * 2**20),
        cost_estimate=pl.CostEstimate(flops=10**6, bytes_accessed=0, transcendentals=0),
    )(
        raw, raw, turned_q, turned_kv, grad, attended, logs, cosine, sine, gains,
        segments[None, :], segments[:, None]
    )


def on_device_fast(
    hidden_in,
    out_grad,
    segment_ids,
    doc_positions,
    attn_gain,
    head_gains,
    w_query,
    w_key,
    w_value,
    w_out,
    ffn_gain,
    w_gate,
    w_up,
    w_down,
):
    low, full = jnp.bfloat16, jnp.float32
    dp, ctx = lax.axis_index("dp"), lax.axis_index("ctx")
    ctx_count = lax.axis_size("ctx")
    core, side, high = dp % 2, dp // 2 % 2, dp // 4
    width = hidden_in.shape[-1]
    rows = w_query.shape[0]
    head = head_gains.shape[0] * lax.axis_size("dp") * ctx_count // 2
    group = w_query.shape[1] // w_key.shape[1]
    kv_own = w_key.shape[1] // head // 2
    units = w_down.shape[0] * ctx_count

    tokens = hidden_in.shape[2]
    marks = jnp.stack(
        [segment_ids[:, 0], doc_positions[:, 0] // 256, doc_positions[:, 0] % 256], 1
    ).reshape(2, 1, -1)
    marks = jnp.pad(marks, ((0, 0), (0, 15), (0, width - 3 * tokens))).astype(low)
    x_came, x_kept = spread(jnp.concatenate([hidden_in[:, 0], marks], 1))

    head_few = head_gains.shape[0]
    gains = jnp.stack([attn_gain, ffn_gain, jnp.pad(head_gains, (0, rows - head_few))])
    gains = jnp.pad(gains, ((0, rows - 3), (0, 128 - rows)))
    key_value = jnp.stack([w_key.reshape(rows, -1, 2, head), w_value.reshape(rows, -1, 2, head)], 3)
    parities = [
        jnp.concatenate(
            [
                w_query.reshape(rows, -1, 2, group * head)[:, :, which].reshape(rows, -1),
                key_value[:, :, which].reshape(rows, -1),
                gains,
            ],
            1,
        )
        for which in range(2)
    ]
    inner = parities[0].shape[1]

    tops = w_gate.shape[1] // units // 4

    def of_member(which):
        return [
            jnp.concatenate(
                [w[:, (top * 4 + which) * units : (top * 4 + which + 1) * units] for top in range(tops)],
                1,
            )
            for w in (w_gate, w_up)
        ]

    def related(zero, one, two, three):
        near, far = choose(side, zero, two), choose(side, two, zero)
        near_far, far_far = choose(side, one, three), choose(side, three, one)
        return (
            choose(core, near, near_far),
            choose(core, far, far_far),
            choose(core, near_far, near),
            choose(core, far_far, far),
        )

    members = [of_member(which) for which in range(4)]
    gate_of = related(*[member[0] for member in members])
    up_of = related(*[member[1] for member in members])
    from_core = flip(
        joined(choose(core, parities[1], parities[0]), gate_of[2], up_of[2], gate_of[3], up_of[3]),
        CORE,
    )
    block = joined(
        choose(core, parities[0], from_core[0]),
        choose(core, from_core[0], parities[1]),
        jnp.pad(w_out, ((0, 0), (0, inner - width))),
    )
    from_side = flip(joined(gate_of[1], up_of[1], from_core[3], from_core[4]), SIDE)
    blocks = [block]
    for step in range(ctx_count - 1):
        blocks.append(spin(blocks[-1]))

    def across(pair):
        return [pair, flip(pair, SIDE), flip(pair, HIGH), flip(pair, SIDE | HIGH)]

    early = across(jnp.concatenate(blocks[:2], 0))
    blocks[3], w_down_late, *early = hold(blocks[3], w_down, *early)
    late = across(jnp.concatenate(blocks[2:], 0))
    block_ffn = unit_block(
        [side * 2 + core, side * 2 + 1 - core, 2 - side * 2 + core, 2 - side * 2 + 1 - core],
        joined(gate_of[0], up_of[0]), from_core, from_side, w_down_late,
    )
    block_ffn, *x_came = hold(block_ffn, *x_came)
    ffn_blocks = [block_ffn, spin(block_ffn)]
    x_half = order(ctx // 2, *settled(x_came, x_kept))
    x_other = flip(x_half, CORE)
    block_ffn, out_late, *late = hold(block_ffn, out_grad, *late)
    ffn_far = [flip(block_ffn, HIGH)]
    df_came, df_kept = spread(out_late[:, 0])
    pieces = [
        pair[3 * part : 3 * part + 3] for pairs in (early, late) for part in range(2) for pair in pairs
    ]

    slots = []
    for step in range(ctx_count):
        place = (ctx - step) % ctx_count
        for far in range(4):
            up = 1 - high if far >= 2 else high
            across_to = 1 - side if far % 2 == 1 else side
            chip = up * 2 + across_to
            slots += [(chip * 2 + c) * ctx_count + place for c in range(2)]
            slots += [chip * ctx_count + place]
    w_in, w_mine = placed(pieces, (0, 0, 1), slots, (8 * ctx_count, 4 * ctx_count))
    w_in, w_mine = w_in.reshape(-1, inner), w_mine.reshape(-1, inner)[:, :width]
    w_in, w_mine, x_other = hold(w_in, w_mine, x_other)
    w_theirs = flip(w_mine, CORE)
    features = inner - 128
    gains_all = w_in[:, features:].reshape(-1, rows, 128)[:, :3, :rows].astype(full)
    w_in = w_in[:, :features]
    attn_gain_all, ffn_gain_all = gains_all[:, 0].reshape(-1), gains_all[:, 1].reshape(-1)
    head_gains_all = gains_all[:, 2, :head_few].reshape(2, head, 1)

    x_all = order(core, x_half, x_other)
    marks = x_all[:, :, tokens, : 3 * tokens].reshape(-1, 3, tokens)
    x_all, x_half = x_all[:, :, :tokens].reshape(-1, width), x_half[:, :tokens].reshape(-1, width)
    segments = marks[:, 0].reshape(-1).astype(jnp.int32)
    places = (256.0 * marks[:, 1].astype(full) + marks[:, 2].astype(full)).reshape(-1)
    normed, _, _ = norm_forward(x_all.astype(full), attn_gain_all)
    a_low = normed.astype(low)
    raw = lax.dot_general(w_in, a_low, (((0,), (1,)), ((), ())), preferred_element_type=full)
    raw, ffn_blocks[1], ffn_far[0], w_theirs = hold(raw, ffn_blocks[1], ffn_far[0], w_theirs)
    ffn_blocks.append(spin(ffn_blocks[1]))
    ffn_far.append(flip(ffn_blocks[1], HIGH))
    freq = THETA ** (-(jnp.arange(head // 2, dtype=full) * 2.0 / head))
    turn = freq[:, None] * places[None, :]
    cosine, sine = jnp.cos(turn), jnp.sin(turn)
    attended, logs, turned_q, turned_kv = attend(
        raw, cosine, sine, head_gains_all, segments, kv_own, head, 256
    )
    attended_low = attended.astype(low)
    o_theirs = flip(half_of(1 - core, attended_low, 1), CORE)
    o_theirs, ffn_blocks[2], ffn_far[1], *df_came = hold(
        o_theirs, ffn_blocks[2], ffn_far[1], *df_came
    )
    df = order(ctx // 2, *settled(df_came, df_kept)).reshape(-1, width)
    df_side, df_core = flip(df, SIDE), flip(df, CORE)
    ffn_blocks.append(spin(ffn_blocks[2]))
    ffn_far.append(flip(ffn_blocks[2], HIGH))
    hidden = (
        x_half.astype(full)
        + left_trans(half_of(core, attended_low, 1), w_mine)
        + left_trans(o_theirs, w_theirs)
    )
    normed_two, h_unit, h_factor = norm_forward(hidden, ffn_gain_all)
    b_own = swap_halves(high, normed_two.astype(low), 1)
    b_own, df_core, ffn_blocks[3], ffn_far[2] = hold(b_own, df_core, ffn_blocks[3], ffn_far[2])
    b_side, b_core = flip(b_own, SIDE), flip(b_own, CORE)
    ffn_far.append(flip(ffn_blocks[3], HIGH))
    b_side, b_core, df_side, ffn_far[3] = hold(b_side, b_core, df_side, ffn_far[3])
    b_both, df_both = flip(b_side, CORE), flip(df_side, CORE)

    units_of = functools.partial(
        feed_forward,
        [(ctx - step) % ctx_count for step in range(ctx_count)] + [high],
        [block for pair in zip(ffn_blocks, ffn_far) for block in pair],
        rows,
    )
    *left, db_side, db_both, out_side, out_both = units_of(
        [b_side, b_both], [df_side, df_both], 256, 2, []
    )
    got_both, got_out_both = flip(db_both, CORE), flip(out_both, CORE)
    db_far = total_low(db_side, got_both)
    block_side = total_low(out_side, got_out_both)
    to_side, b_own, b_core = hold(joined(db_far, block_side), b_own, b_core)
    from_other = flip(to_side, SIDE)
    act, d_pre, team_b, team_df, db_own, db_core, out_own, out_core = units_of(
        [b_own, b_core], [df, df_core], 256, 0, left
    )
    db_core, d_pre, act = hold(db_core, d_pre, act)
    got_core, got_out_core = flip(db_core, CORE), flip(out_core, CORE)

    def behind(step):
        return (ctx - 1 - step) % ctx_count

    g_down = left_trans(act, team_df).astype(low)
    g_down, team_b, from_other, got_core, got_out_core = hold(
        g_down, team_b, from_other, got_core, got_out_core
    )
    got_side, got_block = from_other[0], from_other[1]
    block_out = hidden + out_own.astype(full) + got_out_core.astype(full) + got_block.astype(full)
    block_came, block_kept = unspread(block_out.astype(low).reshape(2, -1, width))

    db = db_own.astype(full) + got_core.astype(full) + got_side.astype(full)
    db = swap_halves(high, db, 1)
    d_hidden, ffn_terms = norm_backward(db, h_unit, h_factor, ffn_gain_all)
    d_hidden = df.astype(full) + d_hidden
    dz = d_hidden.astype(low)
    dz, team_b = hold(dz, team_b)
    dz_other = flip(dz, CORE)
    g_ffn = left_trans(team_b, d_pre).astype(low)
    terms = spread_units(
        [behind(step) for step in range(ctx_count)] + [high], g_ffn, g_down, rows, ctx_count
    )
    *terms, dz_other = hold(*terms, dz_other)
    near_terms = terms[:ctx_count]
    far_got = [flip(term, HIGH) for term in terms[ctx_count:-1]]
    dz_all = order(core, dz, dz_other).reshape(-1, width)
    d_attended = right_trans(w_mine, dz_all).astype(low)
    g_out = matmul(attended_low, dz_all).astype(low).reshape(2, 2, ctx_count, -1, width)

    def side_square(array):
        near = jnp.where(side == 0, array[:, 0], array[:, 1])
        far = jnp.where(side == 0, array[:, 1], array[:, 0])
        near = joined(pick(near, high), pick(near, 1 - high))
        return near, flip(joined(pick(far, high), pick(far, 1 - high)), SIDE)

    def high_square(near, got):
        sums = near.astype(full) + got.astype(full)
        return sums[0], flip(sums[1].astype(low), HIGH)

    def total(terms):
        return functools.reduce(lambda a, b: a + b, [term.astype(full) for term in terms])

    back = functools.partial(
        attend_back, raw, turned_q, turned_kv, attended=attended, logs=logs, cosine=cosine,
        sine=sine, gains=head_gains_all, segments=segments, kv_own=kv_own, head=head, block=256
    )
    g_out = jnp.stack([pick(g_out, behind(step), 2) for step in range(ctx_count)], 2)
    g_out, d_attended = hold(g_out, d_attended)
    out_near, out_got = side_square(g_out)
    dq_one, dkv_one, g_heads_one = back(grad=d_attended, begin=0, count=kv_own // 2)
    dq_one, out_got, far_got[0], d_attended, *block_came = hold(
        dq_one, out_got, far_got[0], d_attended, *block_came
    )
    unit_total = total_low(near_terms[0], far_got[0])
    out_near, out_got = high_square(out_near, out_got)
    d_attended, unit_total = hold(d_attended, unit_total)
    unit_ring = spin(unit_total)
    dq_two, dkv_two, g_heads_two = back(
        grad=d_attended, begin=kv_own // 2, count=kv_own - kv_own // 2
    )
    g_heads = g_heads_one + g_heads_two
    dq_two, unit_ring, far_got[1], out_got, last_term = hold(
        dq_two, unit_ring, far_got[1], out_got, terms[-1]
    )
    far_got.append(flip(last_term, HIGH))
    unit_total = total_low(unit_ring, total_low(near_terms[1], far_got[1]))
    dq_two, unit_total = hold(dq_two, unit_total)
    unit_ring = spin(unit_total)
    d_raw = jnp.concatenate([dq_one, dq_two, dkv_one, dkv_two], 1)
    d_theirs = right_trans(half_of(1 - core, d_raw, 0), w_in).astype(low)
    d_theirs, d_raw = hold(d_theirs, d_raw)
    d_from = flip(d_theirs, CORE)
    d_inner = right_trans(half_of(core, d_raw, 0), w_in)
    d_inner, d_raw = hold(d_inner, d_raw)
    g_in = left_trans(a_low, d_raw).astype(low).reshape(2, 2, 2, ctx_count, rows, features)
    g_in, d_inner, d_from = hold(g_in, d_inner, d_from)
    d_inner = d_inner + d_from.astype(full)
    _, x_unit, x_factor = norm_forward(x_half.astype(full), attn_gain_all)
    d_input, attn_terms = norm_backward(d_inner, x_unit, x_factor, attn_gain_all)
    in_grad = (d_hidden + d_input).astype(low)

    g_gains = jnp.concatenate(
        [
            jnp.sum(attn_terms, 0).reshape(2, 2, 2, ctx_count, rows),
            jnp.sum(ffn_terms, 0).reshape(2, 2, 2, ctx_count, rows),
            g_heads.reshape(2, 2, 2, ctx_count, head_few),
        ],
        -1,
    ).astype(low)
    blank = ((0, 0), (0, 0), (0, 0), (0, 14), (0, width - g_gains.shape[-1]))
    g_gains = jnp.pad(jnp.moveaxis(g_gains, 2, 3), blank)
    g_in = jnp.moveaxis(g_in, 3, 2).reshape(2, 2, ctx_count, 2 * rows, features)
    g_in = jnp.concatenate([g_in, g_gains], 3)
    g_in = jnp.stack([pick(g_in, behind(step), 2) for step in range(ctx_count)], 2)
    g_in, in_grad = hold(g_in, in_grad)
    early_near, early_got = side_square(g_in[:, :, :2])
    late_near, late_got = side_square(g_in[:, :, 2:])
    in_came, in_kept = unspread(in_grad.reshape(2, -1, width))
    out_total = out_near + out_got.astype(full)
    unit_total = total_low(unit_ring, total_low(near_terms[2], far_got[2]))
    unit_ring = spin(unit_total)
    early_near, early_got = high_square(early_near, early_got)
    early_got, late_got, unit_ring, far_got[3] = hold(early_got, late_got, unit_ring, far_got[3])
    unit_total = total_low(unit_ring, total_low(near_terms[3], far_got[3]))
    ffn_total = jnp.concatenate(
        [unit_total[: 4 * rows], unit_total[4 * rows : 8 * rows]], 1
    ).reshape(2, 2, rows, -1)
    g_down = unit_total[8 * rows :, :width]

    found = [
        pick(pick(ffn_total, side), core),
        flip(pick(pick(ffn_total, side), 1 - core), CORE),
        flip(pick(pick(ffn_total, 1 - side), core), SIDE),
        flip(pick(pick(ffn_total, 1 - side), 1 - core), SIDE | CORE),
    ]
    late_near, late_got = high_square(late_near, late_got)

    def terms_of(near, got, first):
        terms = near + got.astype(full)
        return [jnp.concatenate([terms[at], out_total[first + at]], 0) for at in range(2)]

    in_terms = terms_of(early_near, early_got, 0)
    in_ring = spin(in_terms[0].astype(low))
    in_ring, late_got = hold(in_ring, late_got)
    in_terms += terms_of(late_near, late_got, 2)
    in_ring = spin((in_ring.astype(full) + in_terms[1]).astype(low))
    in_ring, *found = hold(in_ring, *found)
    in_ring = spin((in_ring.astype(full) + in_terms[2]).astype(low))
    in_ring, *in_came = hold(in_ring, *in_came)
    found = related(*found)
    found = (found[0], found[2], found[1], found[3])

    def to_columns(first):
        return jnp.concatenate(
            [
                found[which][:, (first + top) * units : (first + top + 1) * units].astype(full)
                for top in range(tops)
                for which in range(4)
            ],
            1,
        )

    g_gate, g_up = to_columns(0), to_columns(tops)

    in_sum = in_ring.astype(full) + in_terms[3]
    g_in, g_out = in_sum[: 2 * rows].astype(low).reshape(2, rows, width), in_sum[2 * rows + 16 :]
    g_gains = in_sum[2 * rows : 2 * rows + 16]
    g_in, *block_came = hold(g_in, *block_came)
    in_grad = order(ctx % 2, *settled(in_came, in_kept))
    block_out = order(ctx % 2, *settled(block_came, block_kept))
    own = pick(g_in, core).astype(full)
    got = flip(jnp.concatenate([pick(g_in, 1 - core), g_gains.astype(low)], 0), CORE).astype(full)
    g_gains = pick(g_gains[:2] + got[rows : rows + 2], core)
    got = got[:rows]
    even, odd = choose(core, own, got), choose(core, got, own)
    first = group * head * kv_own

    def mixed(start, stop, step, size):
        return jnp.concatenate(
            [part[:, at : at + size] for at in range(start, stop, step) for part in (even, odd)], 1
        )

    return (
        block_out[:, None],
        in_grad[:, None],
        g_gains[:rows],
        g_gains[2 * rows : 2 * rows + head_few],
        mixed(0, first, group * head, group * head),
        mixed(first, features, 2 * head, head),
        mixed(first + head, features, 2 * head, head),
        g_out,
        g_gains[rows : 2 * rows],
        g_gate,
        g_up,
        g_down.astype(full),
    )


def solution(mesh):
    placed = (
        P(None, "dp", "ctx", None),
        P(None, "dp", "ctx", None),
        P(None, "dp", "ctx"),
        P(None, "dp", "ctx"),
        P(("dp", "ctx")),
        P(("dp", "ctx")),
        P(("dp", "ctx"), None),
        P(("dp", "ctx"), None),
        P(("dp", "ctx"), None),
        P(("dp", "ctx"), None),
        P(("dp", "ctx")),
        P(("dp", "ctx"), None),
        P(("dp", "ctx"), None),
        P(("dp", "ctx"), None),
    )
    fits = mesh.shape["dp"] == 8 and mesh.shape["ctx"] == 4
    return jax.shard_map(
        on_device_fast if fits else on_device,
        mesh=mesh,
        in_specs=placed,
        out_specs=(
            P(None, "dp", "ctx", None),
            P(None, "dp", "ctx", None),
            P(("dp", "ctx")),
            P(("dp", "ctx")),
            P(("dp", "ctx"), None),
            P(("dp", "ctx"), None),
            P(("dp", "ctx"), None),
            P(("dp", "ctx"), None),
            P(("dp", "ctx")),
            P(("dp", "ctx"), None),
            P(("dp", "ctx"), None),
            P(("dp", "ctx"), None),
        ),
        check_vma=False,
    )
```

profile of v0, /device:TPU:1, one launch (start us, length us, event | category | flops | bytes accessed | tf_op | source)
XLA Modules:
  0.0 453.6 jit_solution(4729225947787456985)
XLA Ops:
  9.0 2.5 collective-permute-start.2
  11.7 3.7 collective-permute-start.8
  15.4 3.7 collective-permute-done.2
  24.3 5.5 %collective-permute-done.3 = bf16[3,32,1152]{2,1,0:T(8,128)(2,1)} collective-permute-done((bf16[3,32,1152]{2,1,0:T(8,128)(2,1)}, bf16[3,32,1152]{2,1,0:T(8,128)(2,1)}, u32[]{:S(2)}, u32[]{:S(2)}) %collective-permute-start.3) | collective-permute-done | bytes 221216 | tf_op jit(solution)/shard_map/ppermute | solution.py:368
  29.7 4.8 %collective-permute-start.9 = (bf16[272,1024]{1,0:T(8,128)(2,1)S(1)}, bf16[272,1024]{1,0:T(8,128)(2,1)}, u32[]{:S(2)}, u32[]{:S(2)}) collective-permute-start(bf16[272,1024]{1,0:T(8,128)(2,1)S(1)} %get-tuple-element.311), channel_id=1, source_target_pairs={{0,2},{1,0},{2,6},{3,4},{4,3},{5,1},{6,7},{7,5},{8,10},{9,8},{10,1... | collective-permute-start | bytes 1671176 | tf_op jit(solution)/shard_map/ppermute | solution.py:608
  38.1 2.8 collective-permute-done.7
  40.8 11.7 %collective-permute-done.4 = bf16[3,32,1152]{2,1,0:T(8,128)(2,1)S(1)} collective-permute-done((bf16[3,32,1152]{2,1,0:T(8,128)(2,1)}, bf16[3,32,1152]{2,1,0:T(8,128)(2,1)S(1)}, u32[]{:S(2)}, u32[]{:S(2)}) %collective-permute-start.4) | collective-permute-done | bytes 221216 | tf_op jit(solution)/shard_map/ppermute | solution.py:368
  56.0 2.3 shard_map.229.refs_0_
  60.5 2.1 collective-permute-start.14
  64.7 1.9 collective-permute-done.11
  66.6 6.8 %collective-permute-done.12 = bf16[6,32,1152]{2,1,0:T(8,128)(2,1)} collective-permute-done((bf16[6,32,1152]{2,1,0:T(8,128)(2,1)S(1)}, bf16[6,32,1152]{2,1,0:T(8,128)(2,1)}, u32[]{:S(2)}, u32[]{:S(2)}) %collective-permute-start.12) | collective-permute-done | bytes 442400 | tf_op jit(solution)/shard_map/ppermute | solution.py:363
  77.9 2.0 collective-permute-start.15
  81.0 3.3 collective-permute-start.20
  84.3 1.6 collective-permute-start.21
  86.0 2.5 slice_convert_fusion
  94.5 2.6 fusion.2
  97.1 4.4 fusion.21.q_ref.kv_ref
  104.0 12.0 %shard_map.231 = (f32[512,1024]{1,0:T(8,128)}, f32[4,2,1024]{2,1,0:T(2,128)}, bf16[512,1024]{1,0:T(8,128)(2,1)}, bf16[512,1024]{1,0:T(8,128)(2,1)}) custom-call(f32[1024,1024]{1,0:T(8,128)} %fusion.21.q_ref.kv_ref, f32[1024,1024]{1,0:T(8,128)} %fusion.21.q_ref.kv_ref, f32[32,1024]{1,0:T(8,128)} %get-tuple-element.433.cos_ref, ...), custom_call_target="tpu_custom_call" | custom-call | flops 1000000 | tf_op jit(solution)/shard_map/pallas_call | solution.py:787
  116.1 1.8 convert_element_type.318
  120.7 6.5 %collective-permute-done.20 = bf16[256,1024]{1,0:T(8,128)(2,1)} collective-permute-done((bf16[256,1024]{1,0:T(8,128)(2,1)}, bf16[256,1024]{1,0:T(8,128)(2,1)}, u32[]{:S(2)}, u32[]{:S(2)}) %collective-permute-start.20) | collective-permute-done | bytes 524320 | tf_op jit(solution)/shard_map/ppermute | solution.py:608
  131.5 2.5 multiply_reduce_fusion.3
  134.8 16.9 %collective-permute-done.23.refs_6_ = bf16[400,1152]{1,0:T(8,128)(2,1)S(1)} collective-permute-done((bf16[400,1152]{1,0:T(8,128)(2,1)}, bf16[400,1152]{1,0:T(8,128)(2,1)S(1)}, u32[]{:S(2)}, u32[]{:S(2)}) %collective-permute-start.23) | collective-permute-done | bytes 921632 | tf_op jit(solution)/shard_map/ppermute | solution.py:368
  154.0 1.9 collective-permute-done.27.refs_10_
  155.9 19.5 %collective-permute-done.28.refs_7_ = bf16[400,1152]{1,0:T(8,128)(2,1)S(1)} collective-permute-done((bf16[400,1152]{1,0:T(8,128)(2,1)S(1)}, bf16[400,1152]{1,0:T(8,128)(2,1)S(1)}, u32[]{:S(2)}, u32[]{:S(2)}) %collective-permute-start.28) | collective-permute-done | bytes 921632 | tf_op jit(solution)/shard_map/ppermute | solution.py:363
  175.4 3.0 collective-permute-done.25.refs_8_
  182.3 1.5 collective-permute-done.30.refs_11_
  183.8 28.0 %shard_map.232 = (bf16[2048,1152]{1,0:T(8,128)(2,1)}, bf16[2048,2304]{1,0:T(8,128)(2,1)}, bf16[2048,1024]{1,0:T(8,128)(2,1)}, bf16[2048,1024]{1,0:T(8,128)(2,1)}...) custom-call(s32[5]{0:T(128)} %stack.296.slots_ref, ...), custom_call_target="tpu_custom_call" | custom-call | flops 6039797760 | tf_op jit(solution)/shard_map/pallas_call | solution.py:516
  212.5 2.4 collective-permute-done.31
  214.8 1.6 fusion.27
  216.9 1.5 pad_maximum_fusion.1
  218.5 27.8 %shard_map.233 = (bf16[2048,1152]{1,0:T(8,128)(2,1)}, bf16[2048,2304]{1,0:T(8,128)(2,1)}, bf16[2048,1024]{1,0:T(8,128)(2,1)}, bf16[2048,1024]{1,0:T(8,128)(2,1)}...) custom-call(s32[5]{0:T(128)} %stack.296.slots_ref, ...), custom_call_target="tpu_custom_call", output_to_operand_aliasing={{0}: (13, {}), {1}: (14, {}), {2}: (15, {}), {3}: (16, {})} | custom-call | flops 6039797760 | tf_op jit(solution)/shard_map/pallas_call | solution.py:516
  247.2 8.8 %convolution_convert_fusion.1.down_ref = bf16[1152,1024]{1,0:T(8,128)(2,1)S(1)} fusion(bf16[2048,1152]{1,0:T(8,128)(2,1)} %get-tuple-element.200, bf16[2048,1024]{1,0:T(8,128)(2,1)} %get-tuple-element.201), kind=kOutput, calls=%fused_computation.7 | convolution fusion | flops 4833017856 | bytes 11272192 | tf_op jit(solution)/shard_map/dot_general | solution.py:19
  255.9 9.6 %collective-permute-done.33 = bf16[2,512,1024]{2,1,0:T(8,128)(2,1)} collective-permute-done((bf16[2,512,1024]{2,1,0:T(8,128)(2,1)}, bf16[2,512,1024]{2,1,0:T(8,128)(2,1)}, u32[]{:S(2)}, u32[]{:S(2)}) %collective-permute-start.33) | collective-permute-done | bytes 2097184 | tf_op jit(solution)/shard_map/ppermute | solution.py:363
  265.6 1.8 convert_add_fusion
  269.0 3.8 fusion.67
  275.1 2.8 collective-permute-start.39
  277.9 3.1 collective-permute-start.40
  281.0 10.4 %convolution_convert_fusion.ffn_ref = bf16[1024,2304]{1,0:T(8,128)(2,1)S(1)} fusion(bf16[2048,1024]{1,0:T(8,128)(2,1)S(1)} %copy-done.23, bf16[2048,2304]{1,0:T(8,128)(2,1)S(1)} %bitcast.314), kind=kOutput, calls=%fused_computation | convolution fusion | flops 9666035712 | bytes 18350080 | tf_op jit(solution)/shard_map/dot_general | solution.py:19
  291.4 2.0 shard_map.234
  296.6 2.3 convolution_convert_fusion.3.do_ref
  302.9 1.5 fusion.15
  305.2 14.8 %shard_map.235 = (bf16[1024,256]{1,0:T(8,128)(2,1)}, bf16[1024,256]{1,0:T(8,128)(2,1)}, f32[2,64,1]{2,1,0:T(8,128)}) custom-call(f32[1024,1024]{1,0:T(8,128)} %fusion.21.q_ref.kv_ref, f32[1024,1024]{1,0:T(8,128)} %fusion.21.q_ref.kv_ref, bf16[512,1024]{1,0:T(8,128)(2,1)} %get-tuple-element.208.qr_ref, bf16[512,1024]{1,0:T(8,128)(2,1)} %get-tuple-element.209.kvr_ref, ...), custom_call_target="tpu_custom_call" | custom-call | flops 1000000 | tf_op jit(solution)/shard_map/pallas_call | solution.py:825
  320.1 3.2 collective-permute-done.38
  323.3 2.3 add_convert_fusion.8
  331.3 14.5 %shard_map.236 = (bf16[1024,256]{1,0:T(8,128)(2,1)}, bf16[1024,256]{1,0:T(8,128)(2,1)}, f32[2,64,1]{2,1,0:T(8,128)}) custom-call(f32[1024,1024]{1,0:T(8,128)} %fusion.21.q_ref.kv_ref, f32[1024,1024]{1,0:T(8,128)} %fusion.21.q_ref.kv_ref, bf16[512,1024]{1,0:T(8,128)(2,1)} %get-tuple-element.208.qr_ref, bf16[512,1024]{1,0:T(8,128)(2,1)} %get-tuple-element.209.kvr_ref, ...), custom_call_target="tpu_custom_call" | custom-call | flops 1000000 | tf_op jit(solution)/shard_map/pallas_call | solution.py:825
  350.1 2.8 add_convert_fusion.6
  358.9 2.4 convolution_convert_fusion.2
  363.6 2.4 fusion.14
  366.0 1.5 copy.67
  369.7 1.9 fusion.3
  373.4 4.2 collective-permute-done.48
  377.6 1.9 add_convert_fusion.4
  380.4 7.8 %collective-permute-done.45 = bf16[2,2,80,1024]{3,2,1,0:T(8,128)(2,1)S(1)} collective-permute-done((bf16[2,2,80,1024]{3,2,1,0:T(8,128)(2,1)S(1)}, bf16[2,2,80,1024]{3,2,1,0:T(8,128)(2,1)S(1)}, u32[]{:S(2)}, u32[]{:S(2)}) %collective-permute-start.45) | collective-permute-done | bytes 655392 | tf_op jit(solution)/shard_map/ppermute | solution.py:363
  390.3 7.0 %collective-permute-start.59 = (bf16[256,1024]{1,0:T(8,128)(2,1)S(1)}, bf16[256,1024]{1,0:T(8,128)(2,1)}, u32[]{:S(2)}, u32[]{:S(2)}) collective-permute-start(bf16[256,1024]{1,0:T(8,128)(2,1)S(1)} %get-tuple-element.314), channel_id=1, source_target_pairs={{1,4},{2,1},{3,5},{4,2},{5,6},{6,3},{9,12},{10,9},{11,13},{12,10},... | collective-permute-start | bytes 1572872 | tf_op jit(solution)/shard_map/ppermute | solution.py:608
  397.3 4.9 %collective-permute-done.47 = bf16[2,2,80,1024]{3,2,1,0:T(8,128)(2,1)S(1)} collective-permute-done((bf16[2,2,80,1024]{3,2,1,0:T(8,128)(2,1)S(1)}, bf16[2,2,80,1024]{3,2,1,0:T(8,128)(2,1)S(1)}, u32[]{:S(2)}, u32[]{:S(2)}) %collective-permute-start.47) | collective-permute-done | bytes 655392 | tf_op jit(solution)/shard_map/ppermute | solution.py:363
  402.9 1.5 add_convert_fusion.2
  408.8 1.5 collective-permute-start.52
  410.3 6.9 %collective-permute-done.52 = bf16[112,1024]{1,0:T(8,128)(2,1)S(1)} collective-permute-done((bf16[112,1024]{1,0:T(8,128)(2,1)S(1)}, bf16[112,1024]{1,0:T(8,128)(2,1)S(1)}, u32[]{:S(2)}, u32[]{:S(2)}) %collective-permute-start.52) | collective-permute-done | bytes 229408 | tf_op jit(solution)/shard_map/ppermute | solution.py:368
  417.3 2.1 collective-permute-start.57
  419.7 2.9 collective-permute-start.60
  423.7 5.0 %collective-permute-done.54 = bf16[112,1024]{1,0:T(8,128)(2,1)S(1)} collective-permute-done((bf16[112,1024]{1,0:T(8,128)(2,1)S(1)}, bf16[112,1024]{1,0:T(8,128)(2,1)S(1)}, u32[]{:S(2)}, u32[]{:S(2)}) %collective-permute-start.54) | collective-permute-done | bytes 229408 | tf_op jit(solution)/shard_map/ppermute | solution.py:368
  431.4 8.2 %collective-permute-done.60 = bf16[256,1024]{1,0:T(8,128)(2,1)S(1)} collective-permute-done((bf16[256,1024]{1,0:T(8,128)(2,1)}, bf16[256,1024]{1,0:T(8,128)(2,1)S(1)}, u32[]{:S(2)}, u32[]{:S(2)}) %collective-permute-start.60) | collective-permute-done | bytes 524320 | tf_op jit(solution)/shard_map/ppermute | solution.py:608
  439.6 5.2 %collective-permute-done.58 = bf16[112,1024]{1,0:T(8,128)(2,1)S(1)} collective-permute-done((bf16[112,1024]{1,0:T(8,128)(2,1)S(1)}, bf16[112,1024]{1,0:T(8,128)(2,1)S(1)}, u32[]{:S(2)}, u32[]{:S(2)}) %collective-permute-start.58) | collective-permute-done | bytes 229408 | tf_op jit(solution)/shard_map/ppermute | solution.py:368
  448.2 1.5 bitcast_dynamic-update-slice_fusion.8
  (426 shorter events, 107.2 us)
Async XLA Ops:
  7.1 1.8 collective-permute-start
  9.0 10.1 %collective-permute-start.2 = (bf16[3,32,1152]{2,1,0:T(8,128)(2,1)S(1)}, bf16[3,32,1152]{2,1,0:T(8,128)(2,1)}, u32[]{:S(2)}, u32[]{:S(2)}) collective-permute-start(bf16[3,32,1152]{2,1,0:T(8,128)(2,1)S(1)} %bitcast_dynamic-update-slice_fusion.12), channel_id=1, source_target_pairs={{0,1},{1,2},{2,3},{3,0},{4,5},{5,6},{6,7},{7,4},{8,9},{9,10},{10,1... | collective-permute-start | bytes 663560 | tf_op jit(solution)/shard_map/ppermute | solution.py:368
  11.7 46.6 %collective-permute-start.8 = (bf16[272,1024]{1,0:T(8,128)(2,1)S(1)}, bf16[272,1024]{1,0:T(8,128)(2,1)S(1)}, u32[]{:S(2)}, u32[]{:S(2)}) collective-permute-start(bf16[272,1024]{1,0:T(8,128)(2,1)S(1)} %get-tuple-element.312), channel_id=1, source_target_pairs={{1,2},{2,4},{3,6},{4,1},{5,3},{6,5},{9,10},{10,12},{11,14},{12,9},... | collective-permute-start | bytes 1671176 | tf_op jit(solution)/shard_map/ppermute | solution.py:608
  20.1 15.0 %collective-permute-start.5 = (bf16[6,32,1152]{2,1,0:T(8,128)(2,1)S(1)}, bf16[6,32,1152]{2,1,0:T(8,128)(2,1)S(1)}, u32[]{:S(2)}, u32[]{:S(2)}) collective-permute-start(bf16[6,32,1152]{2,1,0:T(8,128)(2,1)S(1)} %pad_maximum_fusion.7), channel_id=1, source_target_pairs={{0,8},{4,12},{8,0},{12,4},{16,24},{20,28},{24,16},{28,20},{1,9},{5... | collective-permute-start | bytes 1327112 | tf_op jit(solution)/shard_map/ppermute | solution.py:363
  21.1 14.7 %collective-permute-start.6 = (bf16[6,32,1152]{2,1,0:T(8,128)(2,1)S(1)}, bf16[6,32,1152]{2,1,0:T(8,128)(2,1)S(1)}, u32[]{:S(2)}, u32[]{:S(2)}) collective-permute-start(bf16[6,32,1152]{2,1,0:T(8,128)(2,1)S(1)} %pad_maximum_fusion.7), channel_id=1, source_target_pairs={{0,16},{4,20},{8,24},{12,28},{16,0},{20,4},{24,8},{28,12},{1,17},{... | collective-permute-start | bytes 1327112 | tf_op jit(solution)/shard_map/ppermute | solution.py:363
  22.4 7.3 %collective-permute-start.3 = (bf16[3,32,1152]{2,1,0:T(8,128)(2,1)}, bf16[3,32,1152]{2,1,0:T(8,128)(2,1)}, u32[]{:S(2)}, u32[]{:S(2)}) collective-permute-start(bf16[3,32,1152]{2,1,0:T(8,128)(2,1)} %collective-permute-done.2), channel_id=1, source_target_pairs={{0,1},{1,2},{2,3},{3,0},{4,5},{5,6},{6,7},{7,4},{8,9},{9,10},{10,1... | collective-permute-start | bytes 663560 | tf_op jit(solution)/shard_map/ppermute | solution.py:368
  23.2 17.6 %collective-permute-start.7 = (bf16[6,32,1152]{2,1,0:T(8,128)(2,1)S(1)}, bf16[6,32,1152]{2,1,0:T(8,128)(2,1)S(1)}, u32[]{:S(2)}, u32[]{:S(2)}) collective-permute-start(bf16[6,32,1152]{2,1,0:T(8,128)(2,1)S(1)} %pad_maximum_fusion.7), channel_id=1, source_target_pairs={{0,24},{4,28},{8,16},{12,20},{16,8},{20,12},{24,0},{28,4},{1,25},{... | collective-permute-start | bytes 1327112 | tf_op jit(solution)/shard_map/ppermute | solution.py:363
  29.7 28.6 %collective-permute-start.9 = (bf16[272,1024]{1,0:T(8,128)(2,1)S(1)}, bf16[272,1024]{1,0:T(8,128)(2,1)}, u32[]{:S(2)}, u32[]{:S(2)}) collective-permute-start(bf16[272,1024]{1,0:T(8,128)(2,1)S(1)} %get-tuple-element.311), channel_id=1, source_target_pairs={{0,2},{1,0},{2,6},{3,4},{4,3},{5,1},{6,7},{7,5},{8,10},{9,8},{10,1... | collective-permute-start | bytes 1671176 | tf_op jit(solution)/shard_map/ppermute | solution.py:608
  35.1 19.0 %collective-permute-start.1 = (bf16[4,32,1152]{2,1,0:T(8,128)(2,1)S(1)}, bf16[4,32,1152]{2,1,0:T(8,128)(2,1)S(1)}, u32[]{:S(2)}, u32[]{:S(2)}) collective-permute-start(bf16[4,32,1152]{2,1,0:T(8,128)(2,1)S(1)} %get-tuple-element.371), channel_id=1, source_target_pairs={{0,8},{4,12},{8,0},{12,4},{16,24},{20,28},{24,16},{28,20},{1,9},{5... | collective-permute-start | bytes 884744 | tf_op jit(solution)/shard_map/ppermute | solution.py:363
  35.9 16.7 %collective-permute-start.4 = (bf16[3,32,1152]{2,1,0:T(8,128)(2,1)}, bf16[3,32,1152]{2,1,0:T(8,128)(2,1)S(1)}, u32[]{:S(2)}, u32[]{:S(2)}) collective-permute-start(bf16[3,32,1152]{2,1,0:T(8,128)(2,1)} %collective-permute-done.3), channel_id=1, source_target_pairs={{0,1},{1,2},{2,3},{3,0},{4,5},{5,6},{6,7},{7,4},{8,9},{9,10},{10,1... | collective-permute-start | bytes 663560 | tf_op jit(solution)/shard_map/ppermute | solution.py:368
  52.6 12.2 %collective-permute-start.10 = (bf16[6,32,1152]{2,1,0:T(8,128)(2,1)S(1)}, bf16[6,32,1152]{2,1,0:T(8,128)(2,1)}, u32[]{:S(2)}, u32[]{:S(2)}) collective-permute-start(bf16[6,32,1152]{2,1,0:T(8,128)(2,1)S(1)} %constant_dynamic-update-slice_fusion), channel_id=1, source_target_pairs={{0,8},{4,12},{8,0},{12,4},{16,24},{20,28},{24,16},{28,20},{1,9},{5... | collective-permute-start | bytes 1327112 | tf_op jit(solution)/shard_map/ppermute | solution.py:363
  53.4 13.2 %collective-permute-start.11 = (bf16[6,32,1152]{2,1,0:T(8,128)(2,1)S(1)}, bf16[6,32,1152]{2,1,0:T(8,128)(2,1)}, u32[]{:S(2)}, u32[]{:S(2)}) collective-permute-start(bf16[6,32,1152]{2,1,0:T(8,128)(2,1)S(1)} %constant_dynamic-update-slice_fusion), channel_id=1, source_target_pairs={{0,16},{4,20},{8,24},{12,28},{16,0},{20,4},{24,8},{28,12},{1,17},{... | collective-permute-start | bytes 1327112 | tf_op jit(solution)/shard_map/ppermute | solution.py:363
  54.8 18.6 %collective-permute-start.12 = (bf16[6,32,1152]{2,1,0:T(8,128)(2,1)S(1)}, bf16[6,32,1152]{2,1,0:T(8,128)(2,1)}, u32[]{:S(2)}, u32[]{:S(2)}) collective-permute-start(bf16[6,32,1152]{2,1,0:T(8,128)(2,1)S(1)} %constant_dynamic-update-slice_fusion), channel_id=1, source_target_pairs={{0,24},{4,28},{8,16},{12,20},{16,8},{20,12},{24,0},{28,4},{1,25},{... | collective-permute-start | bytes 1327112 | tf_op jit(solution)/shard_map/ppermute | solution.py:363
  59.8 26.1 %collective-permute-start.13 = (bf16[2,272,1024]{2,1,0:T(8,128)(2,1)S(1)}, bf16[2,272,1024]{2,1,0:T(8,128)(2,1)S(1)}, u32[]{:S(2)}, u32[]{:S(2)}) collective-permute-start(bf16[2,272,1024]{2,1,0:T(8,128)(2,1)S(1)} %bitcast_dynamic-update-slice_fusion.4), channel_id=1, source_target_pairs={{0,4},{4,0},{8,12},{12,8},{16,20},{20,16},{24,28},{28,24},{1,5},{5... | collective-permute-start | bytes 3342344 | tf_op jit(solution)/shard_map/ppermute | solution.py:363
  60.5 41.0 %collective-permute-start.14 = (bf16[400,1152]{1,0:T(8,128)(2,1)}, bf16[400,1152]{1,0:T(8,128)(2,1)}, u32[]{:S(2)}, u32[]{:S(2)}) collective-permute-start(bf16[400,1152]{1,0:T(8,128)(2,1)} %shard_map.229.refs_0_), channel_id=1, source_target_pairs={{0,1},{1,2},{2,3},{3,0},{4,5},{5,6},{6,7},{7,4},{8,9},{9,10},{10,1... | collective-permute-start | bytes 2764808 | tf_op jit(solution)/shard_map/ppermute | solution.py:368
  77.9 23.6 %collective-permute-start.15 = (bf16[400,1152]{1,0:T(8,128)(2,1)}, bf16[400,1152]{1,0:T(8,128)(2,1)}, u32[]{:S(2)}, u32[]{:S(2)}) collective-permute-start(bf16[400,1152]{1,0:T(8,128)(2,1)} %shard_map.229.refs_0_), channel_id=1, source_target_pairs={{0,16},{4,20},{8,24},{12,28},{16,0},{20,4},{24,8},{28,12},{1,17},{... | collective-permute-start | bytes 2764808 | tf_op jit(solution)/shard_map/ppermute | solution.py:363
  81.0 46.2 %collective-permute-start.20 = (bf16[256,1024]{1,0:T(8,128)(2,1)}, bf16[256,1024]{1,0:T(8,128)(2,1)}, u32[]{:S(2)}, u32[]{:S(2)}) collective-permute-start(bf16[256,1024]{1,0:T(8,128)(2,1)} %get-tuple-element.326), channel_id=1, source_target_pairs={{1,2},{2,4},{3,6},{4,1},{5,3},{6,5},{9,10},{10,12},{11,14},{12,9},... | collective-permute-start | bytes 1572872 | tf_op jit(solution)/shard_map/ppermute | solution.py:608
  84.3 42.9 %collective-permute-start.21 = (bf16[256,1024]{1,0:T(8,128)(2,1)}, bf16[256,1024]{1,0:T(8,128)(2,1)}, u32[]{:S(2)}, u32[]{:S(2)}) collective-permute-start(bf16[256,1024]{1,0:T(8,128)(2,1)} %get-tuple-element.325), channel_id=1, source_target_pairs={{0,2},{1,0},{2,6},{3,4},{4,3},{5,1},{6,7},{7,5},{8,10},{9,8},{10,1... | collective-permute-start | bytes 1572872 | tf_op jit(solution)/shard_map/ppermute | solution.py:608
  90.7 10.8 %collective-permute-start.16 = (bf16[512,1024]{1,0:T(8,128)(2,1)}, bf16[512,1024]{1,0:T(8,128)(2,1)}, u32[]{:S(2)}, u32[]{:S(2)}) collective-permute-start(bf16[512,1024]{1,0:T(8,128)(2,1)} %slice.545), channel_id=1, source_target_pairs={{0,4},{4,0},{8,12},{12,8},{16,20},{20,16},{24,28},{28,24},{1,5},{5... | collective-permute-start | bytes 3145736 | tf_op jit(solution)/shard_map/ppermute | solution.py:363
  101.5 25.7 %collective-permute-start.18 = (bf16[400,1152]{1,0:T(8,128)(2,1)}, bf16[400,1152]{1,0:T(8,128)(2,1)}, u32[]{:S(2)}, u32[]{:S(2)}) collective-permute-start(bf16[400,1152]{1,0:T(8,128)(2,1)} %collective-permute-done.14.refs_2_), channel_id=1, source_target_pairs={{0,1},{1,2},{2,3},{3,0},{4,5},{5,6},{6,7},{7,4},{8,9},{9,10},{10,1... | collective-permute-start | bytes 2764808 | tf_op jit(solution)/shard_map/ppermute | solution.py:368
  102.0 25.2 %collective-permute-start.19 = (bf16[400,1152]{1,0:T(8,128)(2,1)}, bf16[400,1152]{1,0:T(8,128)(2,1)}, u32[]{:S(2)}, u32[]{:S(2)}) collective-permute-start(bf16[400,1152]{1,0:T(8,128)(2,1)} %collective-permute-done.14.refs_2_), channel_id=1, source_target_pairs={{0,16},{4,20},{8,24},{12,28},{16,0},{20,4},{24,8},{28,12},{1,17},{... | collective-permute-start | bytes 2764808 | tf_op jit(solution)/shard_map/ppermute | solution.py:363
  118.8 8.4 %collective-permute-start.17 = (bf16[512,512]{1,0:T(8,128)(2,1)}, bf16[512,512]{1,0:T(8,128)(2,1)}, u32[]{:S(2)}, u32[]{:S(2)}) collective-permute-start(bf16[512,512]{1,0:T(8,128)(2,1)} %broadcast_select_fusion.6), channel_id=1, source_target_pairs={{0,4},{4,0},{8,12},{12,8},{16,20},{20,16},{24,28},{28,24},{1,5},{5... | collective-permute-start | bytes 1572872 | tf_op jit(solution)/shard_map/ppermute | solution.py:363
  127.2 24.5 %collective-permute-start.23 = (bf16[400,1152]{1,0:T(8,128)(2,1)}, bf16[400,1152]{1,0:T(8,128)(2,1)S(1)}, u32[]{:S(2)}, u32[]{:S(2)}) collective-permute-start(bf16[400,1152]{1,0:T(8,128)(2,1)} %collective-permute-done.18.refs_4_), channel_id=1, source_target_pairs={{0,1},{1,2},{2,3},{3,0},{4,5},{5,6},{6,7},{7,4},{8,9},{9,10},{10,1... | collective-permute-start | bytes 2764808 | tf_op jit(solution)/shard_map/ppermute | solution.py:368
  127.4 24.3 %collective-permute-start.24 = (bf16[400,1152]{1,0:T(8,128)(2,1)}, bf16[400,1152]{1,0:T(8,128)(2,1)S(1)}, u32[]{:S(2)}, u32[]{:S(2)}) collective-permute-start(bf16[400,1152]{1,0:T(8,128)(2,1)} %collective-permute-done.18.refs_4_), channel_id=1, source_target_pairs={{0,16},{4,20},{8,24},{12,28},{16,0},{20,4},{24,8},{28,12},{1,17},{... | collective-permute-start | bytes 2764808 | tf_op jit(solution)/shard_map/ppermute | solution.py:363
  131.3 20.4 %collective-permute-start.22 = (bf16[512,1024]{1,0:T(8,128)(2,1)S(1)}, bf16[512,1024]{1,0:T(8,128)(2,1)S(1)}, u32[]{:S(2)}, u32[]{:S(2)}) collective-permute-start(bf16[512,1024]{1,0:T(8,128)(2,1)S(1)} %bitcast.310), channel_id=1, source_target_pairs={{0,4},{4,0},{8,12},{12,8},{16,20},{20,16},{24,28},{28,24},{1,5},{5... | collective-permute-start | bytes 3145736 | tf_op jit(solution)/shard_map/ppermute | solution.py:363
  131.4 24.5 %collective-permute-start.27 = (bf16[512,1024]{1,0:T(8,128)(2,1)S(1)}, bf16[512,1024]{1,0:T(8,128)(2,1)}, u32[]{:S(2)}, u32[]{:S(2)}) collective-permute-start(bf16[512,1024]{1,0:T(8,128)(2,1)S(1)} %bitcast.311), channel_id=1, source_target_pairs={{0,8},{4,12},{8,0},{12,4},{16,24},{20,28},{24,16},{28,20},{1,9},{5... | collective-permute-start | bytes 3145736 | tf_op jit(solution)/shard_map/ppermute | solution.py:363
  134.0 134.9 %copy-start.8 = (f32[512,1024]{1,0:T(8,128)}, f32[512,1024]{1,0:T(8,128)S(1)}, u32[]{:S(2)}) copy-start(f32[512,1024]{1,0:T(8,128)S(1)} %get-tuple-element.296) | copy-start | bytes 6291460
  134.0 134.9 %copy-start.55 = (f32[512]{0:T(512)}, f32[512]{0:T(512)S(1)}, u32[]{:S(2)}) copy-start(f32[512]{0:T(512)S(1)} %add_rsqrt_fusion) | copy-start | bytes 6148
  151.8 26.6 %collective-permute-start.25 = (bf16[512,1024]{1,0:T(8,128)(2,1)S(1)}, bf16[512,1024]{1,0:T(8,128)(2,1)}, u32[]{:S(2)}, u32[]{:S(2)}) collective-permute-start(bf16[512,1024]{1,0:T(8,128)(2,1)S(1)} %maximum_select_fusion.1.refs_8_), channel_id=1, source_target_pairs={{0,8},{4,12},{8,0},{12,4},{16,24},{20,28},{24,16},{28,20},{1,9},{5... | collective-permute-start | bytes 3145736 | tf_op jit(solution)/shard_map/ppermute | solution.py:363
  152.5 25.8 %collective-permute-start.26 = (bf16[512,1024]{1,0:T(8,128)(2,1)S(1)}, bf16[512,1024]{1,0:T(8,128)(2,1)S(1)}, u32[]{:S(2)}, u32[]{:S(2)}) collective-permute-start(bf16[512,1024]{1,0:T(8,128)(2,1)S(1)} %maximum_select_fusion.1.refs_8_), channel_id=1, source_target_pairs={{0,4},{4,0},{8,12},{12,8},{16,20},{20,16},{24,28},{28,24},{1,5},{5... | collective-permute-start | bytes 3145736 | tf_op jit(solution)/shard_map/ppermute | solution.py:363
  153.2 22.2 %collective-permute-start.28 = (bf16[400,1152]{1,0:T(8,128)(2,1)S(1)}, bf16[400,1152]{1,0:T(8,128)(2,1)S(1)}, u32[]{:S(2)}, u32[]{:S(2)}) collective-permute-start(bf16[400,1152]{1,0:T(8,128)(2,1)S(1)} %collective-permute-done.23.refs_6_), channel_id=1, source_target_pairs={{0,16},{4,20},{8,24},{12,28},{16,0},{20,4},{24,8},{28,12},{1,17},{... | collective-permute-start | bytes 2764808 | tf_op jit(solution)/shard_map/ppermute | solution.py:363
  178.4 4.0 collective-permute-start.29
  179.7 4.1 collective-permute-start.30
  211.9 2.9 collective-permute-start.31
  212.3 4.1 collective-permute-start.32
  218.4 47.2 %collective-permute-start.33 = (bf16[2,512,1024]{2,1,0:T(8,128)(2,1)}, bf16[2,512,1024]{2,1,0:T(8,128)(2,1)}, u32[]{:S(2)}, u32[]{:S(2)}) collective-permute-start(bf16[2,512,1024]{2,1,0:T(8,128)(2,1)} %pad_maximum_fusion.1), channel_id=1, source_target_pairs={{0,8},{4,12},{8,0},{12,4},{16,24},{20,28},{24,16},{28,20},{1,9},{5... | collective-permute-start | bytes 6291464 | tf_op jit(solution)/shard_map/ppermute | solution.py:363
  246.4 9.6 %collective-permute-start.34 = (bf16[512,1024]{1,0:T(8,128)(2,1)}, bf16[512,1024]{1,0:T(8,128)(2,1)S(1)}, u32[]{:S(2)}, u32[]{:S(2)}) collective-permute-start(bf16[512,1024]{1,0:T(8,128)(2,1)} %get-tuple-element.204), channel_id=1, source_target_pairs={{0,4},{4,0},{8,12},{12,8},{16,20},{20,16},{24,28},{28,24},{1,5},{5... | collective-permute-start | bytes 3145736 | tf_op jit(solution)/shard_map/ppermute | solution.py:363
  247.1 8.9 %collective-permute-start.35 = (bf16[512,1024]{1,0:T(8,128)(2,1)}, bf16[512,1024]{1,0:T(8,128)(2,1)S(1)}, u32[]{:S(2)}, u32[]{:S(2)}) collective-permute-start(bf16[512,1024]{1,0:T(8,128)(2,1)} %get-tuple-element.205), channel_id=1, source_target_pairs={{0,4},{4,0},{8,12},{12,8},{16,20},{20,16},{24,28},{28,24},{1,5},{5... | collective-permute-start | bytes 3145736 | tf_op jit(solution)/shard_map/ppermute | solution.py:363
  272.8 22.5 %collective-permute-start.36 = (bf16[512,1024]{1,0:T(8,128)(2,1)S(1)}, bf16[512,1024]{1,0:T(8,128)(2,1)}, u32[]{:S(2)}, u32[]{:S(2)}) collective-permute-start(bf16[512,1024]{1,0:T(8,128)(2,1)S(1)} %get-tuple-element.213), channel_id=1, source_target_pairs={{0,4},{4,0},{8,12},{12,8},{16,20},{20,16},{24,28},{28,24},{1,5},{5... | collective-permute-start | bytes 3145736 | tf_op jit(solution)/shard_map/ppermute | solution.py:363
  275.1 44.9 %collective-permute-start.39 = (bf16[256,1024]{1,0:T(8,128)(2,1)}, bf16[256,1024]{1,0:T(8,128)(2,1)}, u32[]{:S(2)}, u32[]{:S(2)}) collective-permute-start(bf16[256,1024]{1,0:T(8,128)(2,1)} %get-tuple-element.318), channel_id=1, source_target_pairs={{1,4},{2,1},{3,5},{4,2},{5,6},{6,3},{9,12},{10,9},{11,13},{12,10},... | collective-permute-start | bytes 1572872 | tf_op jit(solution)/shard_map/ppermute | solution.py:608
  277.9 42.2 %collective-permute-start.40 = (bf16[256,1024]{1,0:T(8,128)(2,1)}, bf16[256,1024]{1,0:T(8,128)(2,1)}, u32[]{:S(2)}, u32[]{:S(2)}) collective-permute-start(bf16[256,1024]{1,0:T(8,128)(2,1)} %get-tuple-element.317), channel_id=1, source_target_pairs={{0,1},{1,5},{2,0},{3,4},{4,3},{5,7},{6,2},{7,6},{8,9},{9,13},{10,8... | collective-permute-start | bytes 1572872 | tf_op jit(solution)/shard_map/ppermute | solution.py:608
  300.4 22.9 %collective-permute-start.38 = (bf16[400,1152]{1,0:T(8,128)(2,1)}, bf16[400,1152]{1,0:T(8,128)(2,1)}, u32[]{:S(2)}, u32[]{:S(2)}) collective-permute-start(bf16[400,1152]{1,0:T(8,128)(2,1)} %get-tuple-element.230), channel_id=1, source_target_pairs={{0,16},{4,20},{8,24},{12,28},{16,0},{20,4},{24,8},{28,12},{1,17},{... | collective-permute-start | bytes 2764808 | tf_op jit(solution)/shard_map/ppermute | solution.py:363
  302.2 17.9 %collective-permute-start.37 = (bf16[2,4,32,1024]{3,2,1,0:T(8,128)(2,1)}, bf16[2,4,32,1024]{3,2,1,0:T(8,128)(2,1)}, u32[]{:S(2)}, u32[]{:S(2)}) collective-permute-start(bf16[2,4,32,1024]{3,2,1,0:T(8,128)(2,1)} %pad_maximum_fusion.6), channel_id=1, source_target_pairs={{0,8},{4,12},{8,0},{12,4},{16,24},{20,28},{24,16},{28,20},{1,9},{5... | collective-permute-start | bytes 1572872 | tf_op jit(solution)/shard_map/ppermute | solution.py:363
  304.4 45.6 %collective-permute-start.42 = (bf16[400,1152]{1,0:T(8,128)(2,1)}, bf16[400,1152]{1,0:T(8,128)(2,1)}, u32[]{:S(2)}, u32[]{:S(2)}) collective-permute-start(bf16[400,1152]{1,0:T(8,128)(2,1)} %copy-done.7), channel_id=1, source_target_pairs={{0,16},{4,20},{8,24},{12,28},{16,0},{20,4},{24,8},{28,12},{1,17},{... | collective-permute-start | bytes 2764808 | tf_op jit(solution)/shard_map/ppermute | solution.py:363
  325.6 24.5 %collective-permute-start.41 = (bf16[400,1152]{1,0:T(8,128)(2,1)}, bf16[400,1152]{1,0:T(8,128)(2,1)}, u32[]{:S(2)}, u32[]{:S(2)}) collective-permute-start(bf16[400,1152]{1,0:T(8,128)(2,1)} %add_convert_fusion.8), channel_id=1, source_target_pairs={{0,1},{1,2},{2,3},{3,0},{4,5},{5,6},{6,7},{7,4},{8,9},{9,10},{10,1... | collective-permute-start | bytes 2764808 | tf_op jit(solution)/shard_map/ppermute | solution.py:368
  328.6 21.5 %collective-permute-start.43 = (bf16[4,32,1024]{2,1,0:T(8,128)(2,1)}, bf16[4,32,1024]{2,1,0:T(8,128)(2,1)S(1)}, u32[]{:S(2)}, u32[]{:S(2)}) collective-permute-start(bf16[4,32,1024]{2,1,0:T(8,128)(2,1)} %fusion.47), channel_id=1, source_target_pairs={{0,16},{4,20},{8,24},{12,28},{16,0},{20,4},{24,8},{28,12},{1,17},{... | collective-permute-start | bytes 786440 | tf_op jit(solution)/shard_map/ppermute | solution.py:363
  330.6 42.8 %collective-permute-start.49 = (bf16[400,1152]{1,0:T(8,128)(2,1)}, bf16[400,1152]{1,0:T(8,128)(2,1)}, u32[]{:S(2)}, u32[]{:S(2)}) collective-permute-start(bf16[400,1152]{1,0:T(8,128)(2,1)} %copy-done.6), channel_id=1, source_target_pairs={{0,16},{4,20},{8,24},{12,28},{16,0},{20,4},{24,8},{28,12},{1,17},{... | collective-permute-start | bytes 2764808 | tf_op jit(solution)/shard_map/ppermute | solution.py:363
  352.9 24.6 %collective-permute-start.48 = (bf16[400,1152]{1,0:T(8,128)(2,1)}, bf16[400,1152]{1,0:T(8,128)(2,1)}, u32[]{:S(2)}, u32[]{:S(2)}) collective-permute-start(bf16[400,1152]{1,0:T(8,128)(2,1)} %add_convert_fusion.6), channel_id=1, source_target_pairs={{0,1},{1,2},{2,3},{3,0},{4,5},{5,6},{6,7},{7,4},{8,9},{9,10},{10,1... | collective-permute-start | bytes 2764808 | tf_op jit(solution)/shard_map/ppermute | solution.py:368
  357.2 4.1 collective-permute-start.44
  357.4 39.9 %collective-permute-start.51 = (bf16[400,1152]{1,0:T(8,128)(2,1)S(1)}, bf16[400,1152]{1,0:T(8,128)(2,1)}, u32[]{:S(2)}, u32[]{:S(2)}) collective-permute-start(bf16[400,1152]{1,0:T(8,128)(2,1)S(1)} %copy-done.5), channel_id=1, source_target_pairs={{0,16},{4,20},{8,24},{12,28},{16,0},{20,4},{24,8},{28,12},{1,17},{... | collective-permute-start | bytes 2764808 | tf_op jit(solution)/shard_map/ppermute | solution.py:363
  372.5 15.6 %collective-permute-start.45 = (bf16[2,2,80,1024]{3,2,1,0:T(8,128)(2,1)S(1)}, bf16[2,2,80,1024]{3,2,1,0:T(8,128)(2,1)S(1)}, u32[]{:S(2)}, u32[]{:S(2)}) collective-permute-start(bf16[2,2,80,1024]{3,2,1,0:T(8,128)(2,1)S(1)} %pad_maximum_fusion.3), channel_id=1, source_target_pairs={{0,8},{4,12},{8,0},{12,4},{16,24},{20,28},{24,16},{28,20},{1,9},{5... | collective-permute-start | bytes 1966088 | tf_op jit(solution)/shard_map/ppermute | solution.py:363
  379.4 23.5 %collective-permute-start.50 = (bf16[400,1152]{1,0:T(8,128)(2,1)S(1)}, bf16[400,1152]{1,0:T(8,128)(2,1)S(1)}, u32[]{:S(2)}, u32[]{:S(2)}) collective-permute-start(bf16[400,1152]{1,0:T(8,128)(2,1)S(1)} %add_convert_fusion.4), channel_id=1, source_target_pairs={{0,1},{1,2},{2,3},{3,0},{4,5},{5,6},{6,7},{7,4},{8,9},{9,10},{10,1... | collective-permute-start | bytes 2764808 | tf_op jit(solution)/shard_map/ppermute | solution.py:368
  379.6 22.6 %collective-permute-start.47 = (bf16[2,2,80,1024]{3,2,1,0:T(8,128)(2,1)S(1)}, bf16[2,2,80,1024]{3,2,1,0:T(8,128)(2,1)S(1)}, u32[]{:S(2)}, u32[]{:S(2)}) collective-permute-start(bf16[2,2,80,1024]{3,2,1,0:T(8,128)(2,1)S(1)} %pad_maximum_fusion.4), channel_id=1, source_target_pairs={{0,8},{4,12},{8,0},{12,4},{16,24},{20,28},{24,16},{28,20},{1,9},{5... | collective-permute-start | bytes 1966088 | tf_op jit(solution)/shard_map/ppermute | solution.py:363
  388.5 14.5 %collective-permute-start.46 = (bf16[2,80,1024]{2,1,0:T(8,128)(2,1)S(1)}, bf16[2,80,1024]{2,1,0:T(8,128)(2,1)S(1)}, u32[]{:S(2)}, u32[]{:S(2)}) collective-permute-start(bf16[2,80,1024]{2,1,0:T(8,128)(2,1)S(1)} %fusion.45), channel_id=1, source_target_pairs={{0,16},{4,20},{8,24},{12,28},{16,0},{20,4},{24,8},{28,12},{1,17},{... | collective-permute-start | bytes 983048 | tf_op jit(solution)/shard_map/ppermute | solution.py:363
  390.3 41.1 %collective-permute-start.59 = (bf16[256,1024]{1,0:T(8,128)(2,1)S(1)}, bf16[256,1024]{1,0:T(8,128)(2,1)}, u32[]{:S(2)}, u32[]{:S(2)}) collective-permute-start(bf16[256,1024]{1,0:T(8,128)(2,1)S(1)} %get-tuple-element.314), channel_id=1, source_target_pairs={{1,4},{2,1},{3,5},{4,2},{5,6},{6,3},{9,12},{10,9},{11,13},{12,10},... | collective-permute-start | bytes 1572872 | tf_op jit(solution)/shard_map/ppermute | solution.py:608
  405.5 14.2 %collective-permute-start.55 = (bf16[32,2304]{1,0:T(8,128)(2,1)S(1)}, bf16[32,2304]{1,0:T(8,128)(2,1)S(1)}, u32[]{:S(2)}, u32[]{:S(2)}) collective-permute-start(bf16[32,2304]{1,0:T(8,128)(2,1)S(1)} %get-tuple-element.345), channel_id=1, source_target_pairs={{0,4},{4,0},{8,12},{12,8},{16,20},{20,16},{24,28},{28,24},{1,5},{5... | collective-permute-start | bytes 442376 | tf_op jit(solution)/shard_map/ppermute | solution.py:363
  406.9 15.6 %collective-permute-start.56 = (bf16[32,2304]{1,0:T(8,128)(2,1)S(1)}, bf16[32,2304]{1,0:T(8,128)(2,1)S(1)}, u32[]{:S(2)}, u32[]{:S(2)}) collective-permute-start(bf16[32,2304]{1,0:T(8,128)(2,1)S(1)} %get-tuple-element.344), channel_id=1, source_target_pairs={{0,8},{4,12},{8,0},{12,4},{16,24},{20,28},{24,16},{28,20},{1,9},{5... | collective-permute-start | bytes 442376 | tf_op jit(solution)/shard_map/ppermute | solution.py:363
  408.0 11.4 %collective-permute-start.53 = (bf16[2,80,1024]{2,1,0:T(8,128)(2,1)S(1)}, bf16[2,80,1024]{2,1,0:T(8,128)(2,1)S(1)}, u32[]{:S(2)}, u32[]{:S(2)}) collective-permute-start(bf16[2,80,1024]{2,1,0:T(8,128)(2,1)S(1)} %fusion.46), channel_id=1, source_target_pairs={{0,16},{4,20},{8,24},{12,28},{16,0},{20,4},{24,8},{28,12},{1,17},{... | collective-permute-start | bytes 983048 | tf_op jit(solution)/shard_map/ppermute | solution.py:363
  408.8 8.5 %collective-permute-start.52 = (bf16[112,1024]{1,0:T(8,128)(2,1)S(1)}, bf16[112,1024]{1,0:T(8,128)(2,1)S(1)}, u32[]{:S(2)}, u32[]{:S(2)}) collective-permute-start(bf16[112,1024]{1,0:T(8,128)(2,1)S(1)} %pad_maximum_fusion.8), channel_id=1, source_target_pairs={{0,1},{1,2},{2,3},{3,0},{4,5},{5,6},{6,7},{7,4},{8,9},{9,10},{10,1... | collective-permute-start | bytes 688136 | tf_op jit(solution)/shard_map/ppermute | solution.py:368
  417.3 6.5 %collective-permute-start.57 = (bf16[32,2304]{1,0:T(8,128)(2,1)S(1)}, bf16[32,2304]{1,0:T(8,128)(2,1)S(1)}, u32[]{:S(2)}, u32[]{:S(2)}) collective-permute-start(bf16[32,2304]{1,0:T(8,128)(2,1)S(1)} %get-tuple-element.343), channel_id=1, source_target_pairs={{0,12},{4,8},{8,4},{12,0},{16,28},{20,24},{24,20},{28,16},{1,13},{... | collective-permute-start | bytes 442376 | tf_op jit(solution)/shard_map/ppermute | solution.py:363
  419.4 9.3 %collective-permute-start.54 = (bf16[112,1024]{1,0:T(8,128)(2,1)S(1)}, bf16[112,1024]{1,0:T(8,128)(2,1)S(1)}, u32[]{:S(2)}, u32[]{:S(2)}) collective-permute-start(bf16[112,1024]{1,0:T(8,128)(2,1)S(1)} %fusion.43), channel_id=1, source_target_pairs={{0,1},{1,2},{2,3},{3,0},{4,5},{5,6},{6,7},{7,4},{8,9},{9,10},{10,1... | collective-permute-start | bytes 688136 | tf_op jit(solution)/shard_map/ppermute | solution.py:368
  419.7 19.9 %collective-permute-start.60 = (bf16[256,1024]{1,0:T(8,128)(2,1)}, bf16[256,1024]{1,0:T(8,128)(2,1)S(1)}, u32[]{:S(2)}, u32[]{:S(2)}) collective-permute-start(bf16[256,1024]{1,0:T(8,128)(2,1)} %get-tuple-element.313), channel_id=1, source_target_pairs={{0,1},{1,5},{2,0},{3,4},{4,3},{5,7},{6,2},{7,6},{8,9},{9,13},{10,8... | collective-permute-start | bytes 1572872 | tf_op jit(solution)/shard_map/ppermute | solution.py:608
  429.0 15.8 %collective-permute-start.58 = (bf16[112,1024]{1,0:T(8,128)(2,1)S(1)}, bf16[112,1024]{1,0:T(8,128)(2,1)S(1)}, u32[]{:S(2)}, u32[]{:S(2)}) collective-permute-start(bf16[112,1024]{1,0:T(8,128)(2,1)S(1)} %fusion.44), channel_id=1, source_target_pairs={{0,1},{1,2},{2,3},{3,0},{4,5},{5,6},{6,7},{7,4},{8,9},{9,10},{10,1... | collective-permute-start | bytes 688136 | tf_op jit(solution)/shard_map/ppermute | solution.py:368
  444.9 5.5 %collective-permute-start.61 = (bf16[48,1024]{1,0:T(8,128)(2,1)S(1)}, bf16[48,1024]{1,0:T(8,128)(2,1)S(1)}, u32[]{:S(2)}, u32[]{:S(2)}) collective-permute-start(bf16[48,1024]{1,0:T(8,128)(2,1)S(1)} %pad_maximum_fusion.10), channel_id=1, source_target_pairs={{0,4},{4,0},{8,12},{12,8},{16,20},{20,16},{24,28},{28,24},{1,5},{5... | collective-permute-start | bytes 294920 | tf_op jit(solution)/shard_map/ppermute | solution.py:363
  (74 other events, 558.0 us)
where the time goes:
time: 463 us; the launch traced here: 454 us
  waiting for transfers between devices  144 us (31%)
  Pallas kernels  102 us (22%)
  starting transfers between devices  70.3 us (15%)
  other arithmetic  53 us (11%)
  local copies, waits for them, and re-layouts  45.5 us (10%)
  matrix products  35.3 us (8%)
    ppermute x42, waiting for transfers between devices, flip(): return lax.ppermute(array, 'dp', [(i, i ^ bits) for i in range(count)])  69.8 us
    ppermute x12, waiting for transfers between devices, spin(): lax.ppermute(array, 'ctx', [(i, (i + 1) % count) for i in range(count)])  59.9 us
    pallas_call x2, Pallas kernels, feed_forward(): pl.pallas_call(functools.partial(unit_kernel, mid // 512 * 256, len(piece...  55.9 us
    ppermute x42, starting transfers between devices, flip(): return lax.ppermute(array, 'dp', [(i, i ^ bits) for i in range(count)])  32.8 us
    pallas_call x2, Pallas kernels, attend_back(): pl.pallas_call(functools.partial(backward_kernel, block), grid=(count,),...  29.3 us
    ppermute x8, starting transfers between devices, exchange(): came.append(lax.ppermute(piece, ('dp', 'ctx'), pairs))  29.1 us
    dot_general x5, matrix products, left_trans(): lax.dot_general(left, right, (((0,), (0,)), ((), ())), preferred_element_...  24.8 us
    ppermute x8, waiting for transfers between devices, exchange(): came.append(lax.ppermute(piece, ('dp', 'ctx'), pairs))  14.7 us
  transfers between devices with their start and end apart: 62, of which 27 were waited for; matrix products, arithmetic and copies ran while one was open for 24% of the time, Pallas kernels for 16%

commit v1 on v0

--- a/solution.py
+++ b/solution.py
@@ -1042,24 +1042,19 @@
     got_both, got_out_both = flip(db_both, CORE), flip(out_both, CORE)
     db_far = total_low(db_side, got_both)
     block_side = total_low(out_side, got_out_both)
-    to_side, b_own, b_core = hold(joined(db_far, block_side), b_own, b_core)
-    from_other = flip(to_side, SIDE)
+    db_far, block_side, b_own, b_core = hold(db_far, block_side, b_own, b_core)
+    got_side = flip(db_far, SIDE)
     act, d_pre, team_b, team_df, db_own, db_core, out_own, out_core = units_of(
         [b_own, b_core], [df, df_core], 256, 0, left
     )
-    db_core, d_pre, act = hold(db_core, d_pre, act)
-    got_core, got_out_core = flip(db_core, CORE), flip(out_core, CORE)
+    db_core, d_pre, act, block_side, got_side = hold(db_core, d_pre, act, block_side, got_side)
+    got_core, got_out_core, got_block = flip(db_core, CORE), flip(out_core, CORE), flip(block_side, SIDE)
 
     def behind(step):
         return (ctx - 1 - step) % ctx_count
 
     g_down = left_trans(act, team_df).astype(low)
-    g_down, team_b, from_other, got_core, got_out_core = hold(
-        g_down, team_b, from_other, got_core, got_out_core
-    )
-    got_side, got_block = from_other[0], from_other[1]
-    block_out = hidden + out_own.astype(full) + got_out_core.astype(full) + got_block.astype(full)
-    block_came, block_kept = unspread(block_out.astype(low).reshape(2, -1, width))
+    g_down, team_b, got_core = hold(g_down, team_b, got_core)
 
     db = db_own.astype(full) + got_core.astype(full) + got_side.astype(full)
     db = swap_halves(high, db, 1)
@@ -1069,15 +1064,21 @@
     dz, team_b = hold(dz, team_b)
     dz_other = flip(dz, CORE)
     g_ffn = left_trans(team_b, d_pre).astype(low)
-    terms = spread_units(
-        [behind(step) for step in range(ctx_count)] + [high], g_ffn, g_down, rows, ctx_count
-    )
-    *terms, dz_other = hold(*terms, dz_other)
-    near_terms = terms[:ctx_count]
-    far_got = [flip(term, HIGH) for term in terms[ctx_count:-1]]
+    g_ffn, dz_other = hold(g_ffn, dz_other)
     dz_all = order(core, dz, dz_other).reshape(-1, width)
     d_attended = right_trans(w_mine, dz_all).astype(low)
     g_out = matmul(attended_low, dz_all).astype(low).reshape(2, 2, ctx_count, -1, width)
+    g_out = jnp.stack([pick(g_out, behind(step), 2) for step in range(ctx_count)], 2)
+    terms = spread_units(
+        [behind(step) for step in range(ctx_count)] + [high], g_ffn, g_down, rows, ctx_count
+    )
+    *terms, d_attended, g_out, got_out_core, got_block = hold(
+        *terms, d_attended, g_out, got_out_core, got_block
+    )
+    block_out = hidden + out_own.astype(full) + got_out_core.astype(full) + got_block.astype(full)
+    block_came, block_kept = unspread(block_out.astype(low).reshape(2, -1, width))
+    near_terms = terms[:ctx_count]
+    far_got = [flip(term, HIGH) for term in terms[ctx_count:-1]]
 
     def side_square(array):
         near = jnp.where(side == 0, array[:, 0], array[:, 1])
@@ -1096,8 +1097,6 @@
         attend_back, raw, turned_q, turned_kv, attended=attended, logs=logs, cosine=cosine,
         sine=sine, gains=head_gains_all, segments=segments, kv_own=kv_own, head=head, block=256
     )
-    g_out = jnp.stack([pick(g_out, behind(step), 2) for step in range(ctx_count)], 2)
-    g_out, d_attended = hold(g_out, d_attended)
     out_near, out_got = side_square(g_out)
     dq_one, dkv_one, g_heads_one = back(grad=d_attended, begin=0, count=kv_own // 2)
     dq_one, out_got, far_got[0], d_attended, *block_came = hold(

time: 463 us -> 460 us (level)
  waiting for transfers between devices: 144 us -> 132 us
  starting transfers between devices: 70.3 us -> 77.6 us
    ppermute x42 -> x43, waiting for transfers between devices: 69.8 us -> 61.8 us  [flip(): return lax.ppermute(array, 'dp', [(i, i ^ bits) for i in range(count)])]
    ppermute x12, waiting for transfers between devices: 59.9 us -> 54.9 us  [spin(): lax.ppermute(array, 'ctx', [(i, (i + 1) % count) for i in range(count)])]
    ppermute x42 -> x43, starting transfers between devices: 32.8 us -> 37.1 us  [flip(): return lax.ppermute(array, 'dp', [(i, i ^ bits) for i in range(count)])]
    convert_element_type x4 -> x6, other arithmetic: 8.51 us -> 12.6 us  [total_low(): (left.astype(jnp.float32) + right.astype(jnp.float32)).astype(jnp.bfloat16)]
    unnamed x165 -> x169, local copies, waits for them, and re-layouts: 8.14 us -> 10.7 us
  transfers between devices with their start and end apart: 62 -> 63, of which waited for: 27 -> 24; matrix products, arithmetic and copies ran while one was open for 24% -> 25% of each run, Pallas kernels for 16% -> 17%
where the time goes in v1:
time: 460 us; the launch traced here: 451 us
  waiting for transfers between devices  132 us (29%)
  Pallas kernels  103 us (22%)
  starting transfers between devices  77.6 us (17%)
  other arithmetic  53 us (12%)
  local copies, waits for them, and re-layouts  46.8 us (10%)
  matrix products  35.6 us (8%)
    ppermute x43, waiting for transfers between devices, flip(): return lax.ppermute(array, 'dp', [(i, i ^ bits) for i in range(count)])  61.8 us
    pallas_call x2, Pallas kernels, feed_forward(): pl.pallas_call(functools.partial(unit_kernel, mid // 512 * 256, len(piece...  56 us
    ppermute x12, waiting for transfers between devices, spin(): lax.ppermute(array, 'ctx', [(i, (i + 1) % count) for i in range(count)])  54.9 us
    ppermute x43, starting transfers between devices, flip(): return lax.ppermute(array, 'dp', [(i, i ^ bits) for i in range(count)])  37.1 us
    pallas_call x2, Pallas kernels, attend_back(): pl.pallas_call(functools.partial(backward_kernel, block), grid=(count,),...  29.3 us
    ppermute x8, starting transfers between devices, exchange(): came.append(lax.ppermute(piece, ('dp', 'ctx'), pairs))  29.3 us
    dot_general x5, matrix products, left_trans(): lax.dot_general(left, right, (((0,), (0,)), ((), ())), preferred_element_...  25.1 us
    ppermute x8, waiting for transfers between devices, exchange(): came.append(lax.ppermute(piece, ('dp', 'ctx'), pairs))  15.7 us
  transfers between devices with their start and end apart: 63, of which 24 were waited for; matrix products, arithmetic and copies ran while one was open for 25% of the time, Pallas kernels for 17%

profile of v1, /device:TPU:1, one launch (start us, length us, event | category | flops | bytes accessed | tf_op | source)
XLA Modules:
  0.0 450.6 jit_solution(17640408666145083633)
XLA Ops:
  9.0 2.5 collective-permute-start.2
  11.7 3.7 collective-permute-start.8
  15.4 3.7 collective-permute-done.2
  24.3 5.4 %collective-permute-done.3 = bf16[3,32,1152]{2,1,0:T(8,128)(2,1)} collective-permute-done((bf16[3,32,1152]{2,1,0:T(8,128)(2,1)}, bf16[3,32,1152]{2,1,0:T(8,128)(2,1)}, u32[]{:S(2)}, u32[]{:S(2)}) %collective-permute-start.3) | collective-permute-done | bytes 221216 | tf_op jit(solution)/shard_map/ppermute | solution.py:368
  29.7 4.8 %collective-permute-start.9 = (bf16[272,1024]{1,0:T(8,128)(2,1)S(1)}, bf16[272,1024]{1,0:T(8,128)(2,1)}, u32[]{:S(2)}, u32[]{:S(2)}) collective-permute-start(bf16[272,1024]{1,0:T(8,128)(2,1)S(1)} %get-tuple-element.317), channel_id=1, source_target_pairs={{0,2},{1,0},{2,6},{3,4},{4,3},{5,1},{6,7},{7,5},{8,10},{9,8},{10,1... | collective-permute-start | bytes 1671176 | tf_op jit(solution)/shard_map/ppermute | solution.py:608
  38.1 2.7 collective-permute-done.7
  40.8 11.7 %collective-permute-done.4 = bf16[3,32,1152]{2,1,0:T(8,128)(2,1)S(1)} collective-permute-done((bf16[3,32,1152]{2,1,0:T(8,128)(2,1)}, bf16[3,32,1152]{2,1,0:T(8,128)(2,1)S(1)}, u32[]{:S(2)}, u32[]{:S(2)}) %collective-permute-start.4) | collective-permute-done | bytes 221216 | tf_op jit(solution)/shard_map/ppermute | solution.py:368
  56.0 2.3 shard_map.229.refs_0_
  60.5 2.1 collective-permute-start.14
  64.7 1.9 collective-permute-done.11
  66.6 6.8 %collective-permute-done.12 = bf16[6,32,1152]{2,1,0:T(8,128)(2,1)} collective-permute-done((bf16[6,32,1152]{2,1,0:T(8,128)(2,1)S(1)}, bf16[6,32,1152]{2,1,0:T(8,128)(2,1)}, u32[]{:S(2)}, u32[]{:S(2)}) %collective-permute-start.12) | collective-permute-done | bytes 442400 | tf_op jit(solution)/shard_map/ppermute | solution.py:363
  77.9 2.0 collective-permute-start.15
  81.0 3.3 collective-permute-start.20
  84.3 1.6 collective-permute-start.21
  86.0 2.5 slice_convert_fusion
  94.5 2.6 fusion.2
  97.1 4.3 fusion.20.q_ref.kv_ref
  104.3 12.0 %shard_map.231 = (f32[512,1024]{1,0:T(8,128)}, f32[4,2,1024]{2,1,0:T(2,128)}, bf16[512,1024]{1,0:T(8,128)(2,1)}, bf16[512,1024]{1,0:T(8,128)(2,1)}) custom-call(f32[1024,1024]{1,0:T(8,128)} %fusion.20.q_ref.kv_ref, f32[1024,1024]{1,0:T(8,128)} %fusion.20.q_ref.kv_ref, f32[32,1024]{1,0:T(8,128)} %get-tuple-element.439.cos_ref, ...), custom_call_target="tpu_custom_call" | custom-call | flops 1000000 | tf_op jit(solution)/shard_map/pallas_call | solution.py:787
  116.4 1.8 convert_element_type.312
  121.0 6.1 %collective-permute-done.20 = bf16[256,1024]{1,0:T(8,128)(2,1)} collective-permute-done((bf16[256,1024]{1,0:T(8,128)(2,1)}, bf16[256,1024]{1,0:T(8,128)(2,1)}, u32[]{:S(2)}, u32[]{:S(2)}) %collective-permute-start.20) | collective-permute-done | bytes 524320 | tf_op jit(solution)/shard_map/ppermute | solution.py:608
  127.4 1.5 collective-permute-start.24
  131.5 2.5 multiply_reduce_fusion.3
  134.8 16.6 %collective-permute-done.23.refs_6_ = bf16[400,1152]{1,0:T(8,128)(2,1)S(1)} collective-permute-done((bf16[400,1152]{1,0:T(8,128)(2,1)}, bf16[400,1152]{1,0:T(8,128)(2,1)S(1)}, u32[]{:S(2)}, u32[]{:S(2)}) %collective-permute-start.23) | collective-permute-done | bytes 921632 | tf_op jit(solution)/shard_map/ppermute | solution.py:368
  154.0 1.9 collective-permute-done.27.refs_10_
  155.9 19.5 %collective-permute-done.28.refs_7_ = bf16[400,1152]{1,0:T(8,128)(2,1)S(1)} collective-permute-done((bf16[400,1152]{1,0:T(8,128)(2,1)S(1)}, bf16[400,1152]{1,0:T(8,128)(2,1)S(1)}, u32[]{:S(2)}, u32[]{:S(2)}) %collective-permute-start.28) | collective-permute-done | bytes 921632 | tf_op jit(solution)/shard_map/ppermute | solution.py:363
  175.4 2.9 collective-permute-done.25.refs_8_
  182.3 1.5 collective-permute-done.30.refs_11_
  183.8 28.0 %shard_map.232 = (bf16[2048,1152]{1,0:T(8,128)(2,1)}, bf16[2048,2304]{1,0:T(8,128)(2,1)}, bf16[2048,1024]{1,0:T(8,128)(2,1)}, bf16[2048,1024]{1,0:T(8,128)(2,1)}...) custom-call(s32[5]{0:T(128)} %stack.296.slots_ref, ...), custom_call_target="tpu_custom_call" | custom-call | flops 6039797760 | tf_op jit(solution)/shard_map/pallas_call | solution.py:516
  212.5 2.4 collective-permute-done.32
  214.8 2.6 add_convert_fusion.1
  219.0 28.0 %shard_map.233 = (bf16[2048,1152]{1,0:T(8,128)(2,1)}, bf16[2048,2304]{1,0:T(8,128)(2,1)}, bf16[2048,1024]{1,0:T(8,128)(2,1)}, bf16[2048,1024]{1,0:T(8,128)(2,1)}...) custom-call(s32[5]{0:T(128)} %stack.296.slots_ref, ...), custom_call_target="tpu_custom_call", output_to_operand_aliasing={{0}: (13, {}), {1}: (14, {}), {2}: (15, {}), {3}: (16, {})} | custom-call | flops 6039797760 | tf_op jit(solution)/shard_map/pallas_call | solution.py:516
  249.2 8.6 %convolution_convert_fusion.1.down_ref = bf16[1152,1024]{1,0:T(8,128)(2,1)S(1)} fusion(bf16[2048,1152]{1,0:T(8,128)(2,1)} %get-tuple-element.207, bf16[2048,1024]{1,0:T(8,128)(2,1)} %get-tuple-element.208), kind=kOutput, calls=%fused_computation.7 | convolution fusion | flops 4833017856 | bytes 11272192 | tf_op jit(solution)/shard_map/dot_general | solution.py:19
  257.9 2.0 convert_add_fusion.1
  264.9 10.9 %convolution_convert_fusion.ffn_ref = bf16[1024,2304]{1,0:T(8,128)(2,1)S(1)} fusion(bf16[2048,1024]{1,0:T(8,128)(2,1)S(1)} %copy-done.24, bf16[2048,2304]{1,0:T(8,128)(2,1)S(1)} %bitcast.304), kind=kOutput, calls=%fused_computation | convolution fusion | flops 9666035712 | bytes 18350080 | tf_op jit(solution)/shard_map/dot_general | solution.py:19
  276.2 2.0 shard_map.234
  281.3 2.3 convolution_convert_fusion.4.do_ref
  285.6 2.0 add_convert_fusion
  288.7 4.6 %collective-permute-start.40 = (bf16[256,1024]{1,0:T(8,128)(2,1)}, bf16[256,1024]{1,0:T(8,128)(2,1)}, u32[]{:S(2)}, u32[]{:S(2)}) collective-permute-start(bf16[256,1024]{1,0:T(8,128)(2,1)} %get-tuple-element.324), channel_id=1, source_target_pairs={{1,4},{2,1},{3,5},{4,2},{5,6},{6,3},{9,12},{10,9},{11,13},{12,10},... | collective-permute-start | bytes 1572872 | tf_op jit(solution)/shard_map/ppermute | solution.py:608
  293.3 1.7 collective-permute-start.41
  295.0 1.5 fusion.14
  297.3 14.6 %shard_map.235 = (bf16[1024,256]{1,0:T(8,128)(2,1)}, bf16[1024,256]{1,0:T(8,128)(2,1)}, f32[2,64,1]{2,1,0:T(8,128)}) custom-call(f32[1024,1024]{1,0:T(8,128)} %fusion.20.q_ref.kv_ref, f32[1024,1024]{1,0:T(8,128)} %fusion.20.q_ref.kv_ref, bf16[512,1024]{1,0:T(8,128)(2,1)} %get-tuple-element.232.qr_ref, bf16[512,1024]{1,0:T(8,128)(2,1)} %get-tuple-element.233.kvr_ref, ...), custom_call_target="tpu_custom_call" | custom-call | flops 1000000 | tf_op jit(solution)/shard_map/pallas_call | solution.py:825
  313.4 2.3 add_convert_fusion.9
  315.7 2.5 collective-permute-start.42
  323.8 14.7 %shard_map.236 = (bf16[1024,256]{1,0:T(8,128)(2,1)}, bf16[1024,256]{1,0:T(8,128)(2,1)}, f32[2,64,1]{2,1,0:T(8,128)}) custom-call(f32[1024,1024]{1,0:T(8,128)} %fusion.20.q_ref.kv_ref, f32[1024,1024]{1,0:T(8,128)} %fusion.20.q_ref.kv_ref, bf16[512,1024]{1,0:T(8,128)(2,1)} %get-tuple-element.232.qr_ref, bf16[512,1024]{1,0:T(8,128)(2,1)} %get-tuple-element.233.kvr_ref, ...), custom_call_target="tpu_custom_call" | custom-call | flops 1000000 | tf_op jit(solution)/shard_map/pallas_call | solution.py:825
  338.5 1.5 fusion.48
  342.8 2.8 add_convert_fusion.7
  349.9 4.5 collective-permute-start.45
  355.9 2.4 convolution_convert_fusion.2
  360.6 2.6 fusion.13
  363.2 1.5 copy.67
  366.8 1.9 fusion.3
  370.7 1.9 add_convert_fusion.5
  373.4 12.3 %collective-permute-done.46 = bf16[2,2,80,1024]{3,2,1,0:T(8,128)(2,1)S(1)} collective-permute-done((bf16[2,2,80,1024]{3,2,1,0:T(8,128)(2,1)S(1)}, bf16[2,2,80,1024]{3,2,1,0:T(8,128)(2,1)S(1)}, u32[]{:S(2)}, u32[]{:S(2)}) %collective-permute-start.46) | collective-permute-done | bytes 655392 | tf_op jit(solution)/shard_map/ppermute | solution.py:363
  387.7 6.7 %collective-permute-start.60 = (bf16[256,1024]{1,0:T(8,128)(2,1)S(1)}, bf16[256,1024]{1,0:T(8,128)(2,1)}, u32[]{:S(2)}, u32[]{:S(2)}) collective-permute-start(bf16[256,1024]{1,0:T(8,128)(2,1)S(1)} %get-tuple-element.320), channel_id=1, source_target_pairs={{1,4},{2,1},{3,5},{4,2},{5,6},{6,3},{9,12},{10,9},{11,13},{12,10},... | collective-permute-start | bytes 1572872 | tf_op jit(solution)/shard_map/ppermute | solution.py:608
  394.5 5.3 %collective-permute-done.48 = bf16[2,2,80,1024]{3,2,1,0:T(8,128)(2,1)S(1)} collective-permute-done((bf16[2,2,80,1024]{3,2,1,0:T(8,128)(2,1)S(1)}, bf16[2,2,80,1024]{3,2,1,0:T(8,128)(2,1)S(1)}, u32[]{:S(2)}, u32[]{:S(2)}) %collective-permute-start.48) | collective-permute-done | bytes 655392 | tf_op jit(solution)/shard_map/ppermute | solution.py:363
  399.8 1.5 add_convert_fusion.3
  405.6 1.7 collective-permute-start.53
  407.3 7.3 %collective-permute-done.53 = bf16[112,1024]{1,0:T(8,128)(2,1)S(1)} collective-permute-done((bf16[112,1024]{1,0:T(8,128)(2,1)S(1)}, bf16[112,1024]{1,0:T(8,128)(2,1)S(1)}, u32[]{:S(2)}, u32[]{:S(2)}) %collective-permute-start.53) | collective-permute-done | bytes 229408 | tf_op jit(solution)/shard_map/ppermute | solution.py:368
  414.6 1.8 collective-permute-start.58
  416.7 2.9 collective-permute-start.61
  420.7 5.0 %collective-permute-done.55 = bf16[112,1024]{1,0:T(8,128)(2,1)S(1)} collective-permute-done((bf16[112,1024]{1,0:T(8,128)(2,1)S(1)}, bf16[112,1024]{1,0:T(8,128)(2,1)S(1)}, u32[]{:S(2)}, u32[]{:S(2)}) %collective-permute-start.55) | collective-permute-done | bytes 229408 | tf_op jit(solution)/shard_map/ppermute | solution.py:368
  428.4 8.2 %collective-permute-done.61 = bf16[256,1024]{1,0:T(8,128)(2,1)S(1)} collective-permute-done((bf16[256,1024]{1,0:T(8,128)(2,1)}, bf16[256,1024]{1,0:T(8,128)(2,1)S(1)}, u32[]{:S(2)}, u32[]{:S(2)}) %collective-permute-start.61) | collective-permute-done | bytes 524320 | tf_op jit(solution)/shard_map/ppermute | solution.py:608
  436.6 5.2 %collective-permute-done.59 = bf16[112,1024]{1,0:T(8,128)(2,1)S(1)} collective-permute-done((bf16[112,1024]{1,0:T(8,128)(2,1)S(1)}, bf16[112,1024]{1,0:T(8,128)(2,1)S(1)}, u32[]{:S(2)}, u32[]{:S(2)}) %collective-permute-start.59) | collective-permute-done | bytes 229408 | tf_op jit(solution)/shard_map/ppermute | solution.py:368
  445.2 1.5 bitcast_dynamic-update-slice_fusion.8
  (432 shorter events, 108.5 us)
Async XLA Ops:
  7.1 1.8 collective-permute-start
  9.0 10.1 %collective-permute-start.2 = (bf16[3,32,1152]{2,1,0:T(8,128)(2,1)S(1)}, bf16[3,32,1152]{2,1,0:T(8,128)(2,1)}, u32[]{:S(2)}, u32[]{:S(2)}) collective-permute-start(bf16[3,32,1152]{2,1,0:T(8,128)(2,1)S(1)} %bitcast_dynamic-update-slice_fusion.12), channel_id=1, source_target_pairs={{0,1},{1,2},{2,3},{3,0},{4,5},{5,6},{6,7},{7,4},{8,9},{9,10},{10,1... | collective-permute-start | bytes 663560 | tf_op jit(solution)/shard_map/ppermute | solution.py:368
  11.7 46.6 %collective-permute-start.8 = (bf16[272,1024]{1,0:T(8,128)(2,1)S(1)}, bf16[272,1024]{1,0:T(8,128)(2,1)S(1)}, u32[]{:S(2)}, u32[]{:S(2)}) collective-permute-start(bf16[272,1024]{1,0:T(8,128)(2,1)S(1)} %get-tuple-element.318), channel_id=1, source_target_pairs={{1,2},{2,4},{3,6},{4,1},{5,3},{6,5},{9,10},{10,12},{11,14},{12,9},... | collective-permute-start | bytes 1671176 | tf_op jit(solution)/shard_map/ppermute | solution.py:608
  20.1 15.0 %collective-permute-start.5 = (bf16[6,32,1152]{2,1,0:T(8,128)(2,1)S(1)}, bf16[6,32,1152]{2,1,0:T(8,128)(2,1)S(1)}, u32[]{:S(2)}, u32[]{:S(2)}) collective-permute-start(bf16[6,32,1152]{2,1,0:T(8,128)(2,1)S(1)} %pad_maximum_fusion.6), channel_id=1, source_target_pairs={{0,8},{4,12},{8,0},{12,4},{16,24},{20,28},{24,16},{28,20},{1,9},{5... | collective-permute-start | bytes 1327112 | tf_op jit(solution)/shard_map/ppermute | solution.py:363
  21.1 14.8 %collective-permute-start.6 = (bf16[6,32,1152]{2,1,0:T(8,128)(2,1)S(1)}, bf16[6,32,1152]{2,1,0:T(8,128)(2,1)S(1)}, u32[]{:S(2)}, u32[]{:S(2)}) collective-permute-start(bf16[6,32,1152]{2,1,0:T(8,128)(2,1)S(1)} %pad_maximum_fusion.6), channel_id=1, source_target_pairs={{0,16},{4,20},{8,24},{12,28},{16,0},{20,4},{24,8},{28,12},{1,17},{... | collective-permute-start | bytes 1327112 | tf_op jit(solution)/shard_map/ppermute | solution.py:363
  22.4 7.3 %collective-permute-start.3 = (bf16[3,32,1152]{2,1,0:T(8,128)(2,1)}, bf16[3,32,1152]{2,1,0:T(8,128)(2,1)}, u32[]{:S(2)}, u32[]{:S(2)}) collective-permute-start(bf16[3,32,1152]{2,1,0:T(8,128)(2,1)} %collective-permute-done.2), channel_id=1, source_target_pairs={{0,1},{1,2},{2,3},{3,0},{4,5},{5,6},{6,7},{7,4},{8,9},{9,10},{10,1... | collective-permute-start | bytes 663560 | tf_op jit(solution)/shard_map/ppermute | solution.py:368
  23.2 17.6 %collective-permute-start.7 = (bf16[6,32,1152]{2,1,0:T(8,128)(2,1)S(1)}, bf16[6,32,1152]{2,1,0:T(8,128)(2,1)S(1)}, u32[]{:S(2)}, u32[]{:S(2)}) collective-permute-start(bf16[6,32,1152]{2,1,0:T(8,128)(2,1)S(1)} %pad_maximum_fusion.6), channel_id=1, source_target_pairs={{0,24},{4,28},{8,16},{12,20},{16,8},{20,12},{24,0},{28,4},{1,25},{... | collective-permute-start | bytes 1327112 | tf_op jit(solution)/shard_map/ppermute | solution.py:363
  29.7 28.6 %collective-permute-start.9 = (bf16[272,1024]{1,0:T(8,128)(2,1)S(1)}, bf16[272,1024]{1,0:T(8,128)(2,1)}, u32[]{:S(2)}, u32[]{:S(2)}) collective-permute-start(bf16[272,1024]{1,0:T(8,128)(2,1)S(1)} %get-tuple-element.317), channel_id=1, source_target_pairs={{0,2},{1,0},{2,6},{3,4},{4,3},{5,1},{6,7},{7,5},{8,10},{9,8},{10,1... | collective-permute-start | bytes 1671176 | tf_op jit(solution)/shard_map/ppermute | solution.py:608
  35.2 18.9 %collective-permute-start.1 = (bf16[4,32,1152]{2,1,0:T(8,128)(2,1)S(1)}, bf16[4,32,1152]{2,1,0:T(8,128)(2,1)S(1)}, u32[]{:S(2)}, u32[]{:S(2)}) collective-permute-start(bf16[4,32,1152]{2,1,0:T(8,128)(2,1)S(1)} %get-tuple-element.377), channel_id=1, source_target_pairs={{0,8},{4,12},{8,0},{12,4},{16,24},{20,28},{24,16},{28,20},{1,9},{5... | collective-permute-start | bytes 884744 | tf_op jit(solution)/shard_map/ppermute | solution.py:363
  36.0 16.6 %collective-permute-start.4 = (bf16[3,32,1152]{2,1,0:T(8,128)(2,1)}, bf16[3,32,1152]{2,1,0:T(8,128)(2,1)S(1)}, u32[]{:S(2)}, u32[]{:S(2)}) collective-permute-start(bf16[3,32,1152]{2,1,0:T(8,128)(2,1)} %collective-permute-done.3), channel_id=1, source_target_pairs={{0,1},{1,2},{2,3},{3,0},{4,5},{5,6},{6,7},{7,4},{8,9},{9,10},{10,1... | collective-permute-start | bytes 663560 | tf_op jit(solution)/shard_map/ppermute | solution.py:368
  52.6 12.2 %collective-permute-start.10 = (bf16[6,32,1152]{2,1,0:T(8,128)(2,1)S(1)}, bf16[6,32,1152]{2,1,0:T(8,128)(2,1)}, u32[]{:S(2)}, u32[]{:S(2)}) collective-permute-start(bf16[6,32,1152]{2,1,0:T(8,128)(2,1)S(1)} %constant_dynamic-update-slice_fusion), channel_id=1, source_target_pairs={{0,8},{4,12},{8,0},{12,4},{16,24},{20,28},{24,16},{28,20},{1,9},{5... | collective-permute-start | bytes 1327112 | tf_op jit(solution)/shard_map/ppermute | solution.py:363
  53.4 13.2 %collective-permute-start.11 = (bf16[6,32,1152]{2,1,0:T(8,128)(2,1)S(1)}, bf16[6,32,1152]{2,1,0:T(8,128)(2,1)}, u32[]{:S(2)}, u32[]{:S(2)}) collective-permute-start(bf16[6,32,1152]{2,1,0:T(8,128)(2,1)S(1)} %constant_dynamic-update-slice_fusion), channel_id=1, source_target_pairs={{0,16},{4,20},{8,24},{12,28},{16,0},{20,4},{24,8},{28,12},{1,17},{... | collective-permute-start | bytes 1327112 | tf_op jit(solution)/shard_map/ppermute | solution.py:363
  54.8 18.6 %collective-permute-start.12 = (bf16[6,32,1152]{2,1,0:T(8,128)(2,1)S(1)}, bf16[6,32,1152]{2,1,0:T(8,128)(2,1)}, u32[]{:S(2)}, u32[]{:S(2)}) collective-permute-start(bf16[6,32,1152]{2,1,0:T(8,128)(2,1)S(1)} %constant_dynamic-update-slice_fusion), channel_id=1, source_target_pairs={{0,24},{4,28},{8,16},{12,20},{16,8},{20,12},{24,0},{28,4},{1,25},{... | collective-permute-start | bytes 1327112 | tf_op jit(solution)/shard_map/ppermute | solution.py:363
  59.8 26.1 %collective-permute-start.13 = (bf16[2,272,1024]{2,1,0:T(8,128)(2,1)S(1)}, bf16[2,272,1024]{2,1,0:T(8,128)(2,1)S(1)}, u32[]{:S(2)}, u32[]{:S(2)}) collective-permute-start(bf16[2,272,1024]{2,1,0:T(8,128)(2,1)S(1)} %bitcast_dynamic-update-slice_fusion.4), channel_id=1, source_target_pairs={{0,4},{4,0},{8,12},{12,8},{16,20},{20,16},{24,28},{28,24},{1,5},{5... | collective-permute-start | bytes 3342344 | tf_op jit(solution)/shard_map/ppermute | solution.py:363
  60.5 41.0 %collective-permute-start.14 = (bf16[400,1152]{1,0:T(8,128)(2,1)}, bf16[400,1152]{1,0:T(8,128)(2,1)}, u32[]{:S(2)}, u32[]{:S(2)}) collective-permute-start(bf16[400,1152]{1,0:T(8,128)(2,1)} %shard_map.229.refs_0_), channel_id=1, source_target_pairs={{0,1},{1,2},{2,3},{3,0},{4,5},{5,6},{6,7},{7,4},{8,9},{9,10},{10,1... | collective-permute-start | bytes 2764808 | tf_op jit(solution)/shard_map/ppermute | solution.py:368
  77.9 23.5 %collective-permute-start.15 = (bf16[400,1152]{1,0:T(8,128)(2,1)}, bf16[400,1152]{1,0:T(8,128)(2,1)}, u32[]{:S(2)}, u32[]{:S(2)}) collective-permute-start(bf16[400,1152]{1,0:T(8,128)(2,1)} %shard_map.229.refs_0_), channel_id=1, source_target_pairs={{0,16},{4,20},{8,24},{12,28},{16,0},{20,4},{24,8},{28,12},{1,17},{... | collective-permute-start | bytes 2764808 | tf_op jit(solution)/shard_map/ppermute | solution.py:363
  81.0 46.2 %collective-permute-start.20 = (bf16[256,1024]{1,0:T(8,128)(2,1)}, bf16[256,1024]{1,0:T(8,128)(2,1)}, u32[]{:S(2)}, u32[]{:S(2)}) collective-permute-start(bf16[256,1024]{1,0:T(8,128)(2,1)} %get-tuple-element.332), channel_id=1, source_target_pairs={{1,2},{2,4},{3,6},{4,1},{5,3},{6,5},{9,10},{10,12},{11,14},{12,9},... | collective-permute-start | bytes 1572872 | tf_op jit(solution)/shard_map/ppermute | solution.py:608
  84.3 42.9 %collective-permute-start.21 = (bf16[256,1024]{1,0:T(8,128)(2,1)}, bf16[256,1024]{1,0:T(8,128)(2,1)}, u32[]{:S(2)}, u32[]{:S(2)}) collective-permute-start(bf16[256,1024]{1,0:T(8,128)(2,1)} %get-tuple-element.331), channel_id=1, source_target_pairs={{0,2},{1,0},{2,6},{3,4},{4,3},{5,1},{6,7},{7,5},{8,10},{9,8},{10,1... | collective-permute-start | bytes 1572872 | tf_op jit(solution)/shard_map/ppermute | solution.py:608
  90.7 10.8 %collective-permute-start.16 = (bf16[512,1024]{1,0:T(8,128)(2,1)}, bf16[512,1024]{1,0:T(8,128)(2,1)}, u32[]{:S(2)}, u32[]{:S(2)}) collective-permute-start(bf16[512,1024]{1,0:T(8,128)(2,1)} %slice.537), channel_id=1, source_target_pairs={{0,4},{4,0},{8,12},{12,8},{16,20},{20,16},{24,28},{28,24},{1,5},{5... | collective-permute-start | bytes 3145736 | tf_op jit(solution)/shard_map/ppermute | solution.py:363
  101.5 25.7 %collective-permute-start.18 = (bf16[400,1152]{1,0:T(8,128)(2,1)}, bf16[400,1152]{1,0:T(8,128)(2,1)}, u32[]{:S(2)}, u32[]{:S(2)}) collective-permute-start(bf16[400,1152]{1,0:T(8,128)(2,1)} %collective-permute-done.14.refs_2_), channel_id=1, source_target_pairs={{0,1},{1,2},{2,3},{3,0},{4,5},{5,6},{6,7},{7,4},{8,9},{9,10},{10,1... | collective-permute-start | bytes 2764808 | tf_op jit(solution)/shard_map/ppermute | solution.py:368
  102.4 24.8 %collective-permute-start.19 = (bf16[400,1152]{1,0:T(8,128)(2,1)}, bf16[400,1152]{1,0:T(8,128)(2,1)}, u32[]{:S(2)}, u32[]{:S(2)}) collective-permute-start(bf16[400,1152]{1,0:T(8,128)(2,1)} %collective-permute-done.14.refs_2_), channel_id=1, source_target_pairs={{0,16},{4,20},{8,24},{12,28},{16,0},{20,4},{24,8},{28,12},{1,17},{... | collective-permute-start | bytes 2764808 | tf_op jit(solution)/shard_map/ppermute | solution.py:363
  119.2 8.0 %collective-permute-start.17 = (bf16[512,512]{1,0:T(8,128)(2,1)}, bf16[512,512]{1,0:T(8,128)(2,1)}, u32[]{:S(2)}, u32[]{:S(2)}) collective-permute-start(bf16[512,512]{1,0:T(8,128)(2,1)} %broadcast_select_fusion.6), channel_id=1, source_target_pairs={{0,4},{4,0},{8,12},{12,8},{16,20},{20,16},{24,28},{28,24},{1,5},{5... | collective-permute-start | bytes 1572872 | tf_op jit(solution)/shard_map/ppermute | solution.py:363
  127.2 24.2 %collective-permute-start.23 = (bf16[400,1152]{1,0:T(8,128)(2,1)}, bf16[400,1152]{1,0:T(8,128)(2,1)S(1)}, u32[]{:S(2)}, u32[]{:S(2)}) collective-permute-start(bf16[400,1152]{1,0:T(8,128)(2,1)} %collective-permute-done.18.refs_4_), channel_id=1, source_target_pairs={{0,1},{1,2},{2,3},{3,0},{4,5},{5,6},{6,7},{7,4},{8,9},{9,10},{10,1... | collective-permute-start | bytes 2764808 | tf_op jit(solution)/shard_map/ppermute | solution.py:368
  127.4 24.0 %collective-permute-start.24 = (bf16[400,1152]{1,0:T(8,128)(2,1)}, bf16[400,1152]{1,0:T(8,128)(2,1)S(1)}, u32[]{:S(2)}, u32[]{:S(2)}) collective-permute-start(bf16[400,1152]{1,0:T(8,128)(2,1)} %collective-permute-done.18.refs_4_), channel_id=1, source_target_pairs={{0,16},{4,20},{8,24},{12,28},{16,0},{20,4},{24,8},{28,12},{1,17},{... | collective-permute-start | bytes 2764808 | tf_op jit(solution)/shard_map/ppermute | solution.py:363
  131.3 20.1 %collective-permute-start.22 = (bf16[512,1024]{1,0:T(8,128)(2,1)S(1)}, bf16[512,1024]{1,0:T(8,128)(2,1)S(1)}, u32[]{:S(2)}, u32[]{:S(2)}) collective-permute-start(bf16[512,1024]{1,0:T(8,128)(2,1)S(1)} %bitcast.300), channel_id=1, source_target_pairs={{0,4},{4,0},{8,12},{12,8},{16,20},{20,16},{24,28},{28,24},{1,5},{5... | collective-permute-start | bytes 3145736 | tf_op jit(solution)/shard_map/ppermute | solution.py:363
  131.4 24.5 %collective-permute-start.27 = (bf16[512,1024]{1,0:T(8,128)(2,1)S(1)}, bf16[512,1024]{1,0:T(8,128)(2,1)}, u32[]{:S(2)}, u32[]{:S(2)}) collective-permute-start(bf16[512,1024]{1,0:T(8,128)(2,1)S(1)} %bitcast.301), channel_id=1, source_target_pairs={{0,8},{4,12},{8,0},{12,4},{16,24},{20,28},{24,16},{28,20},{1,9},{5... | collective-permute-start | bytes 3145736 | tf_op jit(solution)/shard_map/ppermute | solution.py:363
  134.0 127.4 %copy-start.8 = (f32[512,1024]{1,0:T(8,128)}, f32[512,1024]{1,0:T(8,128)S(1)}, u32[]{:S(2)}) copy-start(f32[512,1024]{1,0:T(8,128)S(1)} %get-tuple-element.304) | copy-start | bytes 6291460
  151.4 26.9 %collective-permute-start.25 = (bf16[512,1024]{1,0:T(8,128)(2,1)S(1)}, bf16[512,1024]{1,0:T(8,128)(2,1)}, u32[]{:S(2)}, u32[]{:S(2)}) collective-permute-start(bf16[512,1024]{1,0:T(8,128)(2,1)S(1)} %maximum_select_fusion.1.refs_8_), channel_id=1, source_target_pairs={{0,8},{4,12},{8,0},{12,4},{16,24},{20,28},{24,16},{28,20},{1,9},{5... | collective-permute-start | bytes 3145736 | tf_op jit(solution)/shard_map/ppermute | solution.py:363
  152.2 26.1 %collective-permute-start.26 = (bf16[512,1024]{1,0:T(8,128)(2,1)S(1)}, bf16[512,1024]{1,0:T(8,128)(2,1)S(1)}, u32[]{:S(2)}, u32[]{:S(2)}) collective-permute-start(bf16[512,1024]{1,0:T(8,128)(2,1)S(1)} %maximum_select_fusion.1.refs_8_), channel_id=1, source_target_pairs={{0,4},{4,0},{8,12},{12,8},{16,20},{20,16},{24,28},{28,24},{1,5},{5... | collective-permute-start | bytes 3145736 | tf_op jit(solution)/shard_map/ppermute | solution.py:363
  153.2 22.2 %collective-permute-start.28 = (bf16[400,1152]{1,0:T(8,128)(2,1)S(1)}, bf16[400,1152]{1,0:T(8,128)(2,1)S(1)}, u32[]{:S(2)}, u32[]{:S(2)}) collective-permute-start(bf16[400,1152]{1,0:T(8,128)(2,1)S(1)} %collective-permute-done.23.refs_6_), channel_id=1, source_target_pairs={{0,16},{4,20},{8,24},{12,28},{16,0},{20,4},{24,8},{28,12},{1,17},{... | collective-permute-start | bytes 2764808 | tf_op jit(solution)/shard_map/ppermute | solution.py:363
  178.4 4.0 collective-permute-start.29
  179.7 4.1 collective-permute-start.30
  211.9 2.9 collective-permute-start.32
  212.3 5.1 %collective-permute-start.31 = (bf16[512,1024]{1,0:T(8,128)(2,1)}, bf16[512,1024]{1,0:T(8,128)(2,1)S(1)}, u32[]{:S(2)}, u32[]{:S(2)}) collective-permute-start(bf16[512,1024]{1,0:T(8,128)(2,1)} %get-tuple-element.189), channel_id=1, source_target_pairs={{0,4},{4,0},{8,12},{12,8},{16,20},{20,16},{24,28},{28,24},{1,5},{5... | collective-permute-start | bytes 3145736 | tf_op jit(solution)/shard_map/ppermute | solution.py:363
  218.9 28.8 %collective-permute-start.33 = (bf16[512,1024]{1,0:T(8,128)(2,1)}, bf16[512,1024]{1,0:T(8,128)(2,1)}, u32[]{:S(2)}, u32[]{:S(2)}) collective-permute-start(bf16[512,1024]{1,0:T(8,128)(2,1)} %add_convert_fusion.2), channel_id=1, source_target_pairs={{0,8},{4,12},{8,0},{12,4},{16,24},{20,28},{24,16},{28,20},{1,9},{5... | collective-permute-start | bytes 3145736 | tf_op jit(solution)/shard_map/ppermute | solution.py:363
  247.0 36.6 %collective-permute-start.36 = (bf16[512,1024]{1,0:T(8,128)(2,1)}, bf16[512,1024]{1,0:T(8,128)(2,1)S(1)}, u32[]{:S(2)}, u32[]{:S(2)}) collective-permute-start(bf16[512,1024]{1,0:T(8,128)(2,1)} %get-tuple-element.228), channel_id=1, source_target_pairs={{0,4},{4,0},{8,12},{12,8},{16,20},{20,16},{24,28},{28,24},{1,5},{5... | collective-permute-start | bytes 3145736 | tf_op jit(solution)/shard_map/ppermute | solution.py:363
  247.7 10.1 %collective-permute-start.34 = (bf16[512,1024]{1,0:T(8,128)(2,1)}, bf16[512,1024]{1,0:T(8,128)(2,1)S(1)}, u32[]{:S(2)}, u32[]{:S(2)}) collective-permute-start(bf16[512,1024]{1,0:T(8,128)(2,1)} %get-tuple-element.210), channel_id=1, source_target_pairs={{0,4},{4,0},{8,12},{12,8},{16,20},{20,16},{24,28},{28,24},{1,5},{5... | collective-permute-start | bytes 3145736 | tf_op jit(solution)/shard_map/ppermute | solution.py:363
  247.8 35.8 %collective-permute-start.37 = (bf16[512,1024]{1,0:T(8,128)(2,1)S(1)}, bf16[512,1024]{1,0:T(8,128)(2,1)}, u32[]{:S(2)}, u32[]{:S(2)}) collective-permute-start(bf16[512,1024]{1,0:T(8,128)(2,1)S(1)} %copy-done.30), channel_id=1, source_target_pairs={{0,8},{4,12},{8,0},{12,4},{16,24},{20,28},{24,16},{28,20},{1,9},{5... | collective-permute-start | bytes 3145736 | tf_op jit(solution)/shard_map/ppermute | solution.py:363
  262.8 13.3 %collective-permute-start.35 = (bf16[512,1024]{1,0:T(8,128)(2,1)S(1)}, bf16[512,1024]{1,0:T(8,128)(2,1)S(1)}, u32[]{:S(2)}, u32[]{:S(2)}) collective-permute-start(bf16[512,1024]{1,0:T(8,128)(2,1)S(1)} %fusion.64), channel_id=1, source_target_pairs={{0,4},{4,0},{8,12},{12,8},{16,20},{20,16},{24,28},{28,24},{1,5},{5... | collective-permute-start | bytes 3145736 | tf_op jit(solution)/shard_map/ppermute | solution.py:363
  284.6 27.4 %collective-permute-start.38 = (bf16[2,4,32,1024]{3,2,1,0:T(8,128)(2,1)}, bf16[2,4,32,1024]{3,2,1,0:T(8,128)(2,1)}, u32[]{:S(2)}, u32[]{:S(2)}) collective-permute-start(bf16[2,4,32,1024]{3,2,1,0:T(8,128)(2,1)} %pad_maximum_fusion.5), channel_id=1, source_target_pairs={{0,8},{4,12},{8,0},{12,4},{16,24},{20,28},{24,16},{28,20},{1,9},{5... | collective-permute-start | bytes 1572872 | tf_op jit(solution)/shard_map/ppermute | solution.py:363
  284.6 28.7 %collective-permute-start.39 = (bf16[400,1152]{1,0:T(8,128)(2,1)}, bf16[400,1152]{1,0:T(8,128)(2,1)}, u32[]{:S(2)}, u32[]{:S(2)}) collective-permute-start(bf16[400,1152]{1,0:T(8,128)(2,1)} %get-tuple-element.238), channel_id=1, source_target_pairs={{0,16},{4,20},{8,24},{12,28},{16,0},{20,4},{24,8},{28,12},{1,17},{... | collective-permute-start | bytes 2764808 | tf_op jit(solution)/shard_map/ppermute | solution.py:363
  288.7 23.3 %collective-permute-start.40 = (bf16[256,1024]{1,0:T(8,128)(2,1)}, bf16[256,1024]{1,0:T(8,128)(2,1)}, u32[]{:S(2)}, u32[]{:S(2)}) collective-permute-start(bf16[256,1024]{1,0:T(8,128)(2,1)} %get-tuple-element.324), channel_id=1, source_target_pairs={{1,4},{2,1},{3,5},{4,2},{5,6},{6,3},{9,12},{10,9},{11,13},{12,10},... | collective-permute-start | bytes 1572872 | tf_op jit(solution)/shard_map/ppermute | solution.py:608
  293.3 20.0 %collective-permute-start.41 = (bf16[256,1024]{1,0:T(8,128)(2,1)}, bf16[256,1024]{1,0:T(8,128)(2,1)}, u32[]{:S(2)}, u32[]{:S(2)}) collective-permute-start(bf16[256,1024]{1,0:T(8,128)(2,1)} %get-tuple-element.323), channel_id=1, source_target_pairs={{0,1},{1,5},{2,0},{3,4},{4,3},{5,7},{6,2},{7,6},{8,9},{9,13},{10,8... | collective-permute-start | bytes 1572872 | tf_op jit(solution)/shard_map/ppermute | solution.py:608
  296.5 46.2 %collective-permute-start.43 = (bf16[400,1152]{1,0:T(8,128)(2,1)}, bf16[400,1152]{1,0:T(8,128)(2,1)}, u32[]{:S(2)}, u32[]{:S(2)}) collective-permute-start(bf16[400,1152]{1,0:T(8,128)(2,1)} %copy-done.7), channel_id=1, source_target_pairs={{0,16},{4,20},{8,24},{12,28},{16,0},{20,4},{24,8},{28,12},{1,17},{... | collective-permute-start | bytes 2764808 | tf_op jit(solution)/shard_map/ppermute | solution.py:363
  315.7 27.1 %collective-permute-start.42 = (bf16[400,1152]{1,0:T(8,128)(2,1)}, bf16[400,1152]{1,0:T(8,128)(2,1)}, u32[]{:S(2)}, u32[]{:S(2)}) collective-permute-start(bf16[400,1152]{1,0:T(8,128)(2,1)} %add_convert_fusion.9), channel_id=1, source_target_pairs={{0,1},{1,2},{2,3},{3,0},{4,5},{5,6},{6,7},{7,4},{8,9},{9,10},{10,1... | collective-permute-start | bytes 2764808 | tf_op jit(solution)/shard_map/ppermute | solution.py:368
  321.1 21.6 %collective-permute-start.44 = (bf16[4,32,1024]{2,1,0:T(8,128)(2,1)}, bf16[4,32,1024]{2,1,0:T(8,128)(2,1)S(1)}, u32[]{:S(2)}, u32[]{:S(2)}) collective-permute-start(bf16[4,32,1024]{2,1,0:T(8,128)(2,1)} %fusion.44), channel_id=1, source_target_pairs={{0,16},{4,20},{8,24},{12,28},{16,0},{20,4},{24,8},{28,12},{1,17},{... | collective-permute-start | bytes 786440 | tf_op jit(solution)/shard_map/ppermute | solution.py:363
  323.1 47.6 %collective-permute-start.50 = (bf16[400,1152]{1,0:T(8,128)(2,1)}, bf16[400,1152]{1,0:T(8,128)(2,1)}, u32[]{:S(2)}, u32[]{:S(2)}) collective-permute-start(bf16[400,1152]{1,0:T(8,128)(2,1)} %copy-done.6), channel_id=1, source_target_pairs={{0,16},{4,20},{8,24},{12,28},{16,0},{20,4},{24,8},{28,12},{1,17},{... | collective-permute-start | bytes 2764808 | tf_op jit(solution)/shard_map/ppermute | solution.py:363
  345.6 25.1 %collective-permute-start.49 = (bf16[400,1152]{1,0:T(8,128)(2,1)}, bf16[400,1152]{1,0:T(8,128)(2,1)}, u32[]{:S(2)}, u32[]{:S(2)}) collective-permute-start(bf16[400,1152]{1,0:T(8,128)(2,1)} %add_convert_fusion.7), channel_id=1, source_target_pairs={{0,1},{1,2},{2,3},{3,0},{4,5},{5,6},{6,7},{7,4},{8,9},{9,10},{10,1... | collective-permute-start | bytes 2764808 | tf_op jit(solution)/shard_map/ppermute | solution.py:368
  349.9 8.4 %collective-permute-start.45 = (bf16[512,1024]{1,0:T(8,128)(2,1)S(1)}, bf16[512,1024]{1,0:T(8,128)(2,1)S(1)}, u32[]{:S(2)}, u32[]{:S(2)}) collective-permute-start(bf16[512,1024]{1,0:T(8,128)(2,1)S(1)} %fusion.22), channel_id=1, source_target_pairs={{0,4},{4,0},{8,12},{12,8},{16,20},{20,16},{24,28},{28,24},{1,5},{5... | collective-permute-start | bytes 3145736 | tf_op jit(solution)/shard_map/ppermute | solution.py:363
  354.4 40.2 %collective-permute-start.52 = (bf16[400,1152]{1,0:T(8,128)(2,1)S(1)}, bf16[400,1152]{1,0:T(8,128)(2,1)}, u32[]{:S(2)}, u32[]{:S(2)}) collective-permute-start(bf16[400,1152]{1,0:T(8,128)(2,1)S(1)} %copy-done.5), channel_id=1, source_target_pairs={{0,16},{4,20},{8,24},{12,28},{16,0},{20,4},{24,8},{28,12},{1,17},{... | collective-permute-start | bytes 2764808 | tf_op jit(solution)/shard_map/ppermute | solution.py:363
  369.7 16.0 %collective-permute-start.46 = (bf16[2,2,80,1024]{3,2,1,0:T(8,128)(2,1)S(1)}, bf16[2,2,80,1024]{3,2,1,0:T(8,128)(2,1)S(1)}, u32[]{:S(2)}, u32[]{:S(2)}) collective-permute-start(bf16[2,2,80,1024]{3,2,1,0:T(8,128)(2,1)S(1)} %pad_maximum_fusion.2), channel_id=1, source_target_pairs={{0,8},{4,12},{8,0},{12,4},{16,24},{20,28},{24,16},{28,20},{1,9},{5... | collective-permute-start | bytes 1966088 | tf_op jit(solution)/shard_map/ppermute | solution.py:363
  372.6 27.2 %collective-permute-start.51 = (bf16[400,1152]{1,0:T(8,128)(2,1)S(1)}, bf16[400,1152]{1,0:T(8,128)(2,1)S(1)}, u32[]{:S(2)}, u32[]{:S(2)}) collective-permute-start(bf16[400,1152]{1,0:T(8,128)(2,1)S(1)} %add_convert_fusion.5), channel_id=1, source_target_pairs={{0,1},{1,2},{2,3},{3,0},{4,5},{5,6},{6,7},{7,4},{8,9},{9,10},{10,1... | collective-permute-start | bytes 2764808 | tf_op jit(solution)/shard_map/ppermute | solution.py:368
  372.8 27.0 %collective-permute-start.48 = (bf16[2,2,80,1024]{3,2,1,0:T(8,128)(2,1)S(1)}, bf16[2,2,80,1024]{3,2,1,0:T(8,128)(2,1)S(1)}, u32[]{:S(2)}, u32[]{:S(2)}) collective-permute-start(bf16[2,2,80,1024]{3,2,1,0:T(8,128)(2,1)S(1)} %pad_maximum_fusion.3), channel_id=1, source_target_pairs={{0,8},{4,12},{8,0},{12,4},{16,24},{20,28},{24,16},{28,20},{1,9},{5... | collective-permute-start | bytes 1966088 | tf_op jit(solution)/shard_map/ppermute | solution.py:363
  386.0 13.8 %collective-permute-start.47 = (bf16[2,80,1024]{2,1,0:T(8,128)(2,1)S(1)}, bf16[2,80,1024]{2,1,0:T(8,128)(2,1)S(1)}, u32[]{:S(2)}, u32[]{:S(2)}) collective-permute-start(bf16[2,80,1024]{2,1,0:T(8,128)(2,1)S(1)} %fusion.42), channel_id=1, source_target_pairs={{0,16},{4,20},{8,24},{12,28},{16,0},{20,4},{24,8},{28,12},{1,17},{... | collective-permute-start | bytes 983048 | tf_op jit(solution)/shard_map/ppermute | solution.py:363
  387.7 40.6 %collective-permute-start.60 = (bf16[256,1024]{1,0:T(8,128)(2,1)S(1)}, bf16[256,1024]{1,0:T(8,128)(2,1)}, u32[]{:S(2)}, u32[]{:S(2)}) collective-permute-start(bf16[256,1024]{1,0:T(8,128)(2,1)S(1)} %get-tuple-element.320), channel_id=1, source_target_pairs={{1,4},{2,1},{3,5},{4,2},{5,6},{6,3},{9,12},{10,9},{11,13},{12,10},... | collective-permute-start | bytes 1572872 | tf_op jit(solution)/shard_map/ppermute | solution.py:608
  402.4 14.3 %collective-permute-start.56 = (bf16[32,2304]{1,0:T(8,128)(2,1)S(1)}, bf16[32,2304]{1,0:T(8,128)(2,1)S(1)}, u32[]{:S(2)}, u32[]{:S(2)}) collective-permute-start(bf16[32,2304]{1,0:T(8,128)(2,1)S(1)} %get-tuple-element.351), channel_id=1, source_target_pairs={{0,4},{4,0},{8,12},{12,8},{16,20},{20,16},{24,28},{28,24},{1,5},{5... | collective-permute-start | bytes 442376 | tf_op jit(solution)/shard_map/ppermute | solution.py:363
  403.6 15.9 %collective-permute-start.57 = (bf16[32,2304]{1,0:T(8,128)(2,1)S(1)}, bf16[32,2304]{1,0:T(8,128)(2,1)S(1)}, u32[]{:S(2)}, u32[]{:S(2)}) collective-permute-start(bf16[32,2304]{1,0:T(8,128)(2,1)S(1)} %get-tuple-element.350), channel_id=1, source_target_pairs={{0,8},{4,12},{8,0},{12,4},{16,24},{20,28},{24,16},{28,20},{1,9},{5... | collective-permute-start | bytes 442376 | tf_op jit(solution)/shard_map/ppermute | solution.py:363
  405.0 11.4 %collective-permute-start.54 = (bf16[2,80,1024]{2,1,0:T(8,128)(2,1)S(1)}, bf16[2,80,1024]{2,1,0:T(8,128)(2,1)S(1)}, u32[]{:S(2)}, u32[]{:S(2)}) collective-permute-start(bf16[2,80,1024]{2,1,0:T(8,128)(2,1)S(1)} %fusion.43), channel_id=1, source_target_pairs={{0,16},{4,20},{8,24},{12,28},{16,0},{20,4},{24,8},{28,12},{1,17},{... | collective-permute-start | bytes 983048 | tf_op jit(solution)/shard_map/ppermute | solution.py:363
  405.6 9.0 %collective-permute-start.53 = (bf16[112,1024]{1,0:T(8,128)(2,1)S(1)}, bf16[112,1024]{1,0:T(8,128)(2,1)S(1)}, u32[]{:S(2)}, u32[]{:S(2)}) collective-permute-start(bf16[112,1024]{1,0:T(8,128)(2,1)S(1)} %pad_maximum_fusion.7), channel_id=1, source_target_pairs={{0,1},{1,2},{2,3},{3,0},{4,5},{5,6},{6,7},{7,4},{8,9},{9,10},{10,1... | collective-permute-start | bytes 688136 | tf_op jit(solution)/shard_map/ppermute | solution.py:368
  414.6 6.1 %collective-permute-start.58 = (bf16[32,2304]{1,0:T(8,128)(2,1)S(1)}, bf16[32,2304]{1,0:T(8,128)(2,1)S(1)}, u32[]{:S(2)}, u32[]{:S(2)}) collective-permute-start(bf16[32,2304]{1,0:T(8,128)(2,1)S(1)} %get-tuple-element.349), channel_id=1, source_target_pairs={{0,12},{4,8},{8,4},{12,0},{16,28},{20,24},{24,20},{28,16},{1,13},{... | collective-permute-start | bytes 442376 | tf_op jit(solution)/shard_map/ppermute | solution.py:363
  416.4 9.3 %collective-permute-start.55 = (bf16[112,1024]{1,0:T(8,128)(2,1)S(1)}, bf16[112,1024]{1,0:T(8,128)(2,1)S(1)}, u32[]{:S(2)}, u32[]{:S(2)}) collective-permute-start(bf16[112,1024]{1,0:T(8,128)(2,1)S(1)} %fusion.40), channel_id=1, source_target_pairs={{0,1},{1,2},{2,3},{3,0},{4,5},{5,6},{6,7},{7,4},{8,9},{9,10},{10,1... | collective-permute-start | bytes 688136 | tf_op jit(solution)/shard_map/ppermute | solution.py:368
  416.7 19.9 %collective-permute-start.61 = (bf16[256,1024]{1,0:T(8,128)(2,1)}, bf16[256,1024]{1,0:T(8,128)(2,1)S(1)}, u32[]{:S(2)}, u32[]{:S(2)}) collective-permute-start(bf16[256,1024]{1,0:T(8,128)(2,1)} %get-tuple-element.319), channel_id=1, source_target_pairs={{0,1},{1,5},{2,0},{3,4},{4,3},{5,7},{6,2},{7,6},{8,9},{9,13},{10,8... | collective-permute-start | bytes 1572872 | tf_op jit(solution)/shard_map/ppermute | solution.py:608
  426.1 15.7 %collective-permute-start.59 = (bf16[112,1024]{1,0:T(8,128)(2,1)S(1)}, bf16[112,1024]{1,0:T(8,128)(2,1)S(1)}, u32[]{:S(2)}, u32[]{:S(2)}) collective-permute-start(bf16[112,1024]{1,0:T(8,128)(2,1)S(1)} %fusion.41), channel_id=1, source_target_pairs={{0,1},{1,2},{2,3},{3,0},{4,5},{5,6},{6,7},{7,4},{8,9},{9,10},{10,1... | collective-permute-start | bytes 688136 | tf_op jit(solution)/shard_map/ppermute | solution.py:368
  441.9 5.5 %collective-permute-start.62 = (bf16[48,1024]{1,0:T(8,128)(2,1)S(1)}, bf16[48,1024]{1,0:T(8,128)(2,1)S(1)}, u32[]{:S(2)}, u32[]{:S(2)}) collective-permute-start(bf16[48,1024]{1,0:T(8,128)(2,1)S(1)} %pad_maximum_fusion.9), channel_id=1, source_target_pairs={{0,4},{4,0},{8,12},{12,8},{16,20},{20,16},{24,28},{28,24},{1,5},{5... | collective-permute-start | bytes 294920 | tf_op jit(solution)/shard_map/ppermute | solution.py:363
  (77 other events, 684.9 us)
